TPU v7x, 512 devices: a whole 4x4x16 slice. The times are simulated.
512 devices in a mesh: node: 128 (over y, z, core), dp: 4 (over x).
Axes of the slice: x: 4, y: 4, z: 16, core: 2. Of those that a mesh axis runs over, the one named last changes fastest.
Arguments:
- node_feats: bfloat16 [4, 128, 512, 256], P('dp', 'node'), may hold values from -6 to 6
- cotangent: bfloat16 [4, 128, 512, 256], P('dp', 'node'), may hold values from -6 to 6
- mesh_of_block: int32 [4, 128], P('dp', 'node'), may hold values from 0 to 15, as said below
- block_rows: int32 [4, 128], P('dp', 'node'), may hold values from 1 to 512
- ln_gain: float32 [256], replicated, may hold values from 0.5 to 1.5
- w_in_x: bfloat16 [256, 256], replicated, may hold values from -0.375 to 0.375
- w_in_fx: bfloat16 [256, 256], replicated, may hold values from -0.375 to 0.375
- w_slice: float32 [32, 64], replicated, may hold values from -1 to 1
- temper: float32 [8], replicated, may hold values from 0.25 to 1
- w_qkv: float32 [32, 96], replicated, may hold values from -1 to 1
- w_out: bfloat16 [256, 256], replicated, may hold values from -0.375 to 0.375
Outputs:
- feats_grad: bfloat16 [4, 128, 512, 256], P('dp', 'node')
- gain_grad: float32 [256], replicated
- in_x_grad: float32 [256, 256], replicated
- in_fx_grad: float32 [256, 256], replicated
- slice_grad: float32 [32, 64], replicated
- temper_grad: float32 [8], replicated
- qkv_grad: float32 [32, 96], replicated
- out_grad: float32 [256, 256], replicated
Inputs may be any that keep to these rules, and one draw needn't show every extreme that they name: `mesh_of_block`: every mesh number of a group names at least one of its blocks.
All inputs are finite; a program needn't handle non-finite values.
Results may differ from a plain program's by a relative error of at most 0.02.
Values may be sent and summed in bfloat16 or wider, within the bound.
No kernel may reach another device: no remote copies, remote signals or barrier semaphores. Data moves between devices by JAX's collectives and lax.ppermute only.
A program may use at most 64 MiB of HBM per device.

v0:
```python
import math

import jax
import jax.numpy as jnp
from jax import lax
from jax.sharding import PartitionSpec as P

MESH_G = 16


EPS_NORM = 1e-05
EPS_MASS = 1e-05


def build_masks(ids, rows, meshes, length):
    valid = (jnp.arange(length, dtype=jnp.int32)[None, :] < rows[:, None]).astype(jnp.float32)
    onehot = (ids[:, None] == jnp.arange(meshes, dtype=jnp.int32)[None, :]).astype(jnp.float32)
    return (valid, onehot)


def layer_norm(xf, ln_gain):
    mean = jnp.mean(xf, axis=-1, keepdims=True)
    centered = xf - mean
    var = jnp.mean(centered * centered, axis=-1, keepdims=True)
    return (centered * lax.rsqrt(var + EPS_NORM) * ln_gain).astype(jnp.bfloat16)


def slice_softmax(logits, temper, valid):
    heads = temper.shape[0]
    shape = logits.shape
    scaled = logits.reshape(shape[:-1] + (heads, shape[-1] // heads)) / temper[:, None]
    expo = jnp.exp(scaled)
    weights = expo / jnp.sum(expo, axis=-1, keepdims=True) * valid[..., None, None]
    weights = weights.reshape(shape)
    return (weights, weights.astype(jnp.bfloat16))


def to_blockdiag(values, heads):
    blocks, _, slices, head_size = values.shape
    identity = jnp.eye(heads, dtype=values.dtype)
    expanded = values[:, :, :, None, :] * identity[None, :, None, :, None]
    return expanded.reshape(blocks, heads * slices, heads * head_size)


def take_diagonal(full, heads):
    blocks, total, width = full.shape
    shaped = full.reshape(blocks, heads, total // heads, heads, width // heads)
    head_ids = jnp.arange(heads, dtype=jnp.int32)
    return jnp.moveaxis(shaped[:, head_ids, :, head_ids, :], 0, 1)


def collect_sums(sw, feat, weights, onehot, heads):
    blocks, rows, total = sw.shape
    slices = total // heads
    head_size = feat.shape[-1] // heads
    full = jnp.einsum("bnk,bnc->bkc", sw, feat, preferred_element_type=jnp.float32)
    per_block = take_diagonal(full, heads)
    mass_block = jnp.sum(weights, axis=1).reshape(blocks, heads, slices)
    table = jnp.einsum("bk,bhmd->khmd", onehot, per_block, precision=lax.Precision.HIGHEST)
    mass = jnp.einsum("bk,bhm->khm", onehot, mass_block, precision=lax.Precision.HIGHEST)
    return (table.reshape(-1, slices, head_size), mass.reshape(-1, slices))


def collect_back(sw, feat, onehot, d_table, d_mass, heads):
    blocks, rows, total = sw.shape
    slices = total // heads
    head_size = feat.shape[-1] // heads
    d_block = jnp.einsum(
        "bk,khmd->bhmd",
        onehot,
        d_table.reshape(-1, heads, slices, head_size),
        precision=lax.Precision.HIGHEST,
    )
    d_diag = to_blockdiag(d_block, heads)
    d_sw_b = jnp.einsum(
        "bnc,bkc->bnk", feat.astype(jnp.float32), d_diag, precision=lax.Precision.HIGHEST
    ).astype(jnp.bfloat16)
    d_feat = jnp.einsum(
        "bnk,bkc->bnc", sw.astype(jnp.float32), d_diag, precision=lax.Precision.HIGHEST
    ).astype(jnp.bfloat16)
    d_mass_block = jnp.einsum(
        "bk,khm->bhm", onehot, d_mass.reshape(-1, heads, slices), precision=lax.Precision.HIGHEST
    )
    d_weights = jnp.broadcast_to(d_mass_block.reshape(blocks, 1, total), (blocks, rows, total))
    return (d_sw_b, d_feat, d_weights)


def attend(table, mass, w_qkv):
    width = table.shape[-1]
    token = table / (mass[..., None] + EPS_MASS)
    qkv = jnp.einsum("pmd,de->pme", token, w_qkv, precision=lax.Precision.HIGHEST)
    query = qkv[..., :width]
    keys = qkv[..., width : 2 * width]
    values = qkv[..., 2 * width :]
    scores = jnp.einsum("pmd,pnd->pmn", query, keys, precision=lax.Precision.HIGHEST) / math.sqrt(
        width
    )
    expo = jnp.exp(scores)
    probs = expo / jnp.sum(expo, axis=-1, keepdims=True)
    mixed = jnp.einsum("pmn,pnd->pmd", probs, values, precision=lax.Precision.HIGHEST)
    return mixed.astype(jnp.bfloat16)


def choose_tokens(mixed, onehot, heads):
    slices = mixed.shape[1]
    head_size = mixed.shape[2]
    chosen = jnp.einsum(
        "bk,khmd->bhmd",
        onehot,
        mixed.astype(jnp.float32).reshape(-1, heads, slices, head_size),
        precision=lax.Precision.HIGHEST,
    )
    return to_blockdiag(chosen.astype(jnp.bfloat16), heads)


def deslice_out(sw, chosen_diag):
    out = jnp.einsum("bnk,bkc->bnc", sw, chosen_diag, preferred_element_type=jnp.float32)
    return out.astype(jnp.bfloat16)


def deslice_back(sw, chosen_diag, onehot, d_out, heads):
    blocks, rows, total = sw.shape
    slices = total // heads
    head_size = d_out.shape[-1] // heads
    d_sw_a = jnp.einsum(
        "bnc,bkc->bnk", d_out, chosen_diag, preferred_element_type=jnp.float32
    ).astype(jnp.bfloat16)
    d_full = jnp.einsum("bnk,bnc->bkc", sw, d_out, preferred_element_type=jnp.float32)
    d_chosen = take_diagonal(d_full, heads)
    d_mixed_f = jnp.einsum("bk,bhmd->khmd", onehot, d_chosen, precision=lax.Precision.HIGHEST)
    return (d_sw_a, d_mixed_f.reshape(-1, slices, head_size))


def contract_rows(left, right):
    flat_left = left.reshape(-1, left.shape[-1])
    flat_right = right.reshape(-1, right.shape[-1])
    return lax.dot_general(
        flat_left, flat_right, (((0,), (0,)), ((), ())), preferred_element_type=jnp.float32
    )


def contract_last(left, right):
    return lax.dot_general(
        left, right, (((2,), (1,)), ((), ())), preferred_element_type=jnp.float32
    )


def front(xf, valid, onehot, ln_gain, w_in_x, w_in_fx, w_slice, temper):
    heads = temper.shape[0]
    normed, ln_pull = jax.vjp(layer_norm, xf, ln_gain)
    mid = jnp.dot(normed, w_in_x, preferred_element_type=jnp.float32).astype(jnp.bfloat16)
    feat = jnp.dot(normed, w_in_fx, preferred_element_type=jnp.float32).astype(jnp.bfloat16)
    blockdiag = jnp.kron(jnp.eye(heads, dtype=jnp.float32), w_slice).astype(jnp.bfloat16)
    logits = jnp.dot(mid, blockdiag, preferred_element_type=jnp.float32)
    (weights, sw), soft_pull = jax.vjp(lambda lg, tp: slice_softmax(lg, tp, valid), logits, temper)
    sw = lax.optimization_barrier(sw)
    table, mass = collect_sums(sw, feat, weights, onehot, heads)
    saved = (normed, ln_pull, mid, blockdiag, soft_pull, feat, onehot, sw)
    return (table, mass, saved)


def back(saved, d_sw_a, d_table, d_mass, g, w_in_x, w_in_fx, heads):
    normed, ln_pull, mid, blockdiag, soft_pull, feat, onehot, sw = saved
    heads_total = blockdiag.shape[1]
    width = blockdiag.shape[0]
    d_sw_b, d_feat, d_weights = collect_back(sw, feat, onehot, d_table, d_mass, heads)
    d_sw = (d_sw_a.astype(jnp.float32) + d_sw_b.astype(jnp.float32)).astype(jnp.bfloat16)
    d_logits, temper_grad = soft_pull((d_weights, d_sw))
    d_logits = d_logits.astype(jnp.bfloat16)
    slices = heads_total // heads
    head_size = width // heads
    d_block = contract_rows(mid, d_logits).reshape(heads, head_size, heads, slices)
    head_ids = jnp.arange(heads, dtype=jnp.int32)
    slice_grad = jnp.sum(d_block[head_ids, :, head_ids, :], axis=0)
    d_mid = contract_last(d_logits, blockdiag).astype(jnp.bfloat16)
    in_x_grad = contract_rows(normed, d_mid)
    in_fx_grad = contract_rows(normed, d_feat)
    d_normed = (contract_last(d_mid, w_in_x) + contract_last(d_feat, w_in_fx)).astype(jnp.bfloat16)
    d_ln, gain_grad = ln_pull(d_normed)
    feats_grad = (g + d_ln).astype(jnp.bfloat16)
    return (feats_grad, gain_grad, in_x_grad, in_fx_grad, slice_grad, temper_grad)


def shards(
    node_feats,
    cotangent,
    mesh_of_block,
    block_rows,
    ln_gain,
    w_in_x,
    w_in_fx,
    w_slice,
    temper,
    w_qkv,
    w_out,
):
    heads = temper.shape[0]
    blocks_here = node_feats[0]
    length = blocks_here.shape[1]
    valid, onehot = build_masks(mesh_of_block[0], block_rows[0], MESH_G, length)
    xf = blocks_here.astype(jnp.float32)
    table, mass, saved = front(xf, valid, onehot, ln_gain, w_in_x, w_in_fx, w_slice, temper)
    sw = saved[7]
    full_table, full_mass = lax.psum((table, mass), "node")
    mixed, attend_pull = jax.vjp(attend, full_table, full_mass, w_qkv)
    mixed = lax.optimization_barrier(mixed)
    chosen_diag = choose_tokens(mixed, onehot, heads)
    out = deslice_out(sw, chosen_diag)
    g = cotangent[0].astype(jnp.float32) * valid[..., None]
    g_b = g.astype(jnp.bfloat16)
    out_grad = contract_rows(out, g_b)
    d_out = contract_last(g_b, w_out).astype(jnp.bfloat16)
    d_sw_a, d_mixed_f = deslice_back(sw, chosen_diag, onehot, d_out, heads)
    total_grad = lax.psum(d_mixed_f, "node")
    d_table, d_mass, qkv_grad = attend_pull(total_grad.astype(jnp.bfloat16))
    qkv_grad = qkv_grad * (lax.axis_index("node") == 0).astype(jnp.float32)
    feats_grad, gain_grad, in_x_grad, in_fx_grad, slice_grad, temper_grad = back(
        saved, d_sw_a, d_table, d_mass, g, w_in_x, w_in_fx, heads
    )
    gain_grad, in_x_grad, in_fx_grad, slice_grad, temper_grad, qkv_grad, out_grad = lax.psum(
        (gain_grad, in_x_grad, in_fx_grad, slice_grad, temper_grad, qkv_grad, out_grad),
        ("node", "dp"),
    )
    return (
        feats_grad[None],
        gain_grad,
        in_x_grad,
        in_fx_grad,
        slice_grad,
        temper_grad,
        qkv_grad,
        out_grad,
    )


def solution(mesh):
    placed = (
        P("dp", "node", None, None),
        P("dp", "node", None, None),
        P("dp", "node"),
        P("dp", "node"),
        P(),
        P(),
        P(),
        P(),
        P(),
        P(),
        P(),
    )
    return jax.shard_map(
        shards,
        mesh=mesh,
        in_specs=placed,
        out_specs=(P("dp", "node", None, None), P(), P(), P(), P(), P(), P(), P()),
        check_vma=False,
    )
```

profile of v0, /device:TPU:1, one launch (start us, length us, event | category | flops | bytes accessed | tf_op | source)
XLA Modules:
  0.0 1143.4 jit_solution(12808544771690245722)
XLA Ops:
  12.9 1.7 convolution_convert_fusion.6
  22.6 2.9 broadcast_multiply_fusion
  31.1 523.0 %all-reduce.13 = (f32[128,64]{1,0:T(8,128)}, bf16[128,64,32]{1,2,0:T(8,128)(2,1)}) all-reduce(f32[128,64]{1,0:T(8,128)} %multiply_bitcast_fusion, f32[128,64,32]{1,2,0:T(8,128)S(1)} %bitcast.214), channel_id=1, replica_groups=mesh['node'=128,'dp'=4] {'node'}, use_global_device_ids=true, to_apply=%region_5.6 | all-reduce | flops 270336 | bytes 1638400 | tf_op jit(solution)/shard_map/psum | solution.py:204
  557.5 1.9 broadcast_divide_fusion.1
  559.4 2.6 copy.98
  562.0 3.9 fusion.53
  565.9 1.7 fusion.78
  567.6 4.0 copy.100
  571.6 4.1 copy.99
  575.7 11.5 %fusion.3 = (f32[128,64]{1,0:T(8,128)S(1)}, f32[128,64,64]{1,2,0:T(8,128)}) fusion(f32[128,64,32]{1,2,0:T(8,128)} %copy.99, f32[128,64,32]{1,2,0:T(8,128)} %copy.100), kind=kOutput, calls=%fused_computation.10 | convolution fusion | flops 202366976 | bytes 4227072 | tf_op jit(solution)/shard_map/jvp(pmd,pnd->pmn)/dot_general | solution.py:95
  588.5 4.0 copy.102
  592.6 7.1 multiply_reduce_fusion
  599.7 4.9 fusion.76
  604.7 7.6 fusion.77
  612.3 3.8 fusion.15
  616.2 5.7 convolution_convert_fusion
  621.9 4.8 multiply_reduce_fusion.1
  626.8 2.0 fusion.4
  630.0 2.3 mul.356
  632.2 2.7 fusion.11
  635.0 2.6 convolution_convert_fusion.8
  637.6 1.9 fusion.23
  641.4 2.1 mul.352
  650.3 1.8 fusion.10
  653.2 1.8 multiply_reduce_fusion.2
  658.3 2.5 fusion.17
  660.7 1.9 fusion.70
  666.9 2.4 fusion.83
  671.3 1.8 gather_fusion.2
  674.0 8.4 fusion.19
  682.4 104.9 %all-reduce.3 = (f32[256]{0:T(256)}, f32[32,64]{1,0:T(8,128)}, f32[8]{0:T(128)}, f32[32,96]{1,0:T(8,128)}) all-reduce(f32[256]{0:T(256)S(1)} %copy-done.34, f32[32,64]{1,0:T(8,128)S(1)} %reduce_sum.146, f32[8]{0:T(128)S(1)} %neg.37, f32[32,96]{1,0:T(8,128)S(1)} %fusion.19), channel_id=1, replica_groups=mesh['node'=128,'dp'=4] {'node','dp'}, use_global_device_ids=true, to_apply=%region_14.15 | all-reduce | flops 5384 | bytes 43072 | tf_op jit(solution)/shard_map/psum | solution.py:220
  787.4 343.8 %all-reduce.12.cloned.1.call-done = (f32[256,256]{1,0:T(8,128)}, f32[256,256]{1,0:T(8,128)}, f32[256,256]{1,0:T(8,128)}) async-done(((f32[256,256]{1,0:T(8,128)}, f32[256,256]{1,0:T(8,128)}, f32[256,256]{1,0:T(8,128)}), (f32[256,256]{1,0:T(8,128)}, f32[256,256]{1,0:T(8,128)}, f32[256,256]{1,0:T(8,128)})) %all-reduce.12.cloned.1.call-update) | async-done | bytes 786448 | tf_op jit(solution)/shard_map/psum | solution.py:220
  (136 shorter events, 48.7 us)
Async XLA Ops:
  7.2 5.8 copy-start
  7.2 8.5 copy-start.33
  7.2 550.3 %all-reduce.10.cloned.1.call-start = ((), (), s32[]{:S(2)}) async-start(), calls=%async_computation | async-start | bytes 4194304 | tf_op jit(solution)/shard_map/psum | solution.py:204
  8.4 10.2 copy-start.9
  8.4 9.9 copy-start.24
  9.8 5.5 copy-start.27
  11.6 8.1 copy-start.10
  16.0 3.7 copy-start.22
  16.1 3.6 copy-start.30
  16.1 3.6 copy-start.17
  17.1 2.6 copy-start.2
  25.6 1105.5 %all-reduce.12.cloned.1.call-start = ((), (), s32[]{:S(2)}) async-start(), calls=%async_computation.1 | async-start | bytes 1572864 | tf_op jit(solution)/shard_map/psum | solution.py:220
  592.5 7.1 copy-start.1
  592.5 7.1 copy-start.4
  592.6 7.2 copy-start.21
  599.7 5.0 copy-start.5
  604.7 17.2 %copy-start.13 = (f32[128,64,32]{1,2,0:T(8,128)}, f32[128,64,32]{1,2,0:T(8,128)S(1)}, u32[]{:S(2)}) copy-start(f32[128,64,32]{1,2,0:T(8,128)S(1)} %fusion.76) | copy-start | bytes 3145732
  604.7 7.6 copy-start.16
  612.3 9.6 copy-start.14
  612.3 3.8 copy-start.3
  616.2 5.7 copy-start.15
  616.2 5.7 copy-start.12
  616.2 5.7 copy-start.19
  616.2 5.7 copy-start.26
  616.2 5.7 copy-start.31
  649.4 3.8 copy-start.23
  649.4 6.5 copy-start.11
  650.3 5.9 copy-start.25
  650.3 7.0 copy-start.28
  650.3 7.0 copy-start.32
  656.2 10.7 copy-start.7
  674.0 8.4 copy-start.34
  (5 other events, 5.1 us)
Sparse Core Ops, SparseCore 0:
  25.7 353.3 all-reduce.9
  669.4 461.6 all-reduce.11
where the time goes:
time: 1150 us; the launch traced here: 1140 us
  blocking collectives  628 us (55%)
  waiting for transfers between devices  344 us (30%)
  matrix products  84.9 us (7%)
  local copies, waits for them, and re-layouts  45.6 us (4%)
  other arithmetic  24.8 us (2%)
  between operations  16.4 us (1%)
    psum x1, blocking collectives, shards(): full_table, full_mass = lax.psum((table, mass), 'node')  523 us
    psum x1, waiting for transfers between devices, shards(): lax.psum((gain_grad, in_x_grad, in_fx_grad, slice_grad, temper_grad, qkv_...  344 us
    psum x1, blocking collectives, shards(): lax.psum((gain_grad, in_x_grad, in_fx_grad, slice_grad, temper_grad, qkv_...  105 us
    dot_general x3, matrix products, attend(): jnp.einsum('pmd,pnd->pmn', query, keys, precision=lax.Precision.HIGHEST)  24.1 us
  transfers between devices with their start and end apart: 2, of which 1 were waited for; matrix products, arithmetic and copies ran while one was open for 2% of the time, Pallas kernels for 0%

commit v1 on v0

v1 whole, which is shorter than its diff:
```python
import math

import jax
import jax.numpy as jnp
from jax import lax
from jax.experimental import pallas as pl
from jax.experimental.pallas import tpu as pltpu
from jax.sharding import Mesh
from jax.sharding import PartitionSpec as P

EPS_NORM = 1e-05
EPS_MASS = 1e-05
HEADS = 8
DH = 32
SLICES = 64
WIDTH = 256
ROWS = 512
OWNERS = 8
PEERS = 32
SHARE = 8
BF16_MAX = 3.3895313892515355e38
F32 = jnp.float32
BF16 = jnp.bfloat16
HIGHEST = lax.Precision.HIGHEST


def iota(shape, dim):
    return lax.broadcasted_iota(jnp.int32, shape, dim)


def dot(a, b, dims=((1,), (0,)), precision=None):
    return lax.dot_general(a, b, (dims, ((), ())), precision=precision, preferred_element_type=F32)


def four_blocks(w_slice):
    two = jnp.concatenate([w_slice, w_slice], axis=1)
    four = jnp.concatenate([two, two], axis=1)
    tall = jnp.concatenate([four] * 4, axis=0)
    same = (iota((128, 256), 0) >> 5) == (iota((128, 256), 1) >> 6)
    return jnp.where(same, tall, 0.0).astype(BF16)


def head_ones():
    return ((iota((256, 256), 0) >> 6) == (iota((256, 256), 1) >> 6)).astype(F32).astype(BF16)


def fold_matrix():
    return ((iota((128, 128), 0) & 31) == (iota((128, 128), 1) & 31)).astype(F32).astype(BF16)


def quarter_mask(rows):
    return ((iota((rows, 128), 0) & 63) >> 4) == (iota((rows, 128), 1) >> 5)


def pack_rows(tiled):
    rows = tiled.shape[0]
    kept = jnp.where(quarter_mask(rows), tiled, 0.0)
    return jnp.sum(kept.reshape(rows // 64, 4, 16, 128), axis=1)


def spread_rows(packed):
    heads = packed.shape[0]
    tall = jnp.broadcast_to(packed[:, None], (heads, 4, 16, 128)).reshape(heads * 64, 128)
    return jnp.where(quarter_mask(heads * 64), tall, 0.0)


def temper_row(temper, group):
    head = iota((1, 256), 1) >> 6
    row = jnp.zeros((1, 256), F32)
    for i in range(4):
        row = jnp.where(head == i, temper[:, 4 * group + i : 4 * group + i + 1], row)
    return row


def head_sums(values, ones):
    high = jnp.clip(values, -BF16_MAX, BF16_MAX).astype(BF16)
    low = (values - high.astype(F32)).astype(BF16)
    return dot(high, ones) + dot(low, ones)


def weights_of(mid, blocks, inv_temper, ones, valid):
    scaled = dot(mid, blocks) * inv_temper
    expo = jnp.exp(scaled)
    return scaled, expo / head_sums(expo, ones) * valid


def valid_column(rows_ref):
    return (iota((ROWS, 1), 0) < rows_ref[0]).astype(F32)


def normalise(x):
    xf = x.astype(F32)
    mean = jnp.mean(xf, axis=-1, keepdims=True)
    centered = xf - mean
    var = jnp.mean(centered * centered, axis=-1, keepdims=True)
    rstd = lax.rsqrt(var + EPS_NORM)
    return centered * rstd, rstd


def front_kernel(
    rows_ref, mesh_ref, x_hbm, gain_hbm, wx_hbm, wfx_hbm, slice_hbm, temper_hbm, cot_hbm, wout_hbm,
    send_ref, normed_ref, mid_ref, feat_ref, sw_ref, dout_ref, scaled_ref, weights_ref, xhat_ref, rstd_ref,
    gain_ref, wx_ref, wfx_ref, cot_ref, blocks_ref, temper_ref,
    x_ref, slice_ref, heat_ref, wout_ref, sems,
):
    sources = (x_hbm, gain_hbm, wx_hbm, wfx_hbm, slice_hbm, temper_hbm, cot_hbm, wout_hbm)
    targets = (x_ref, gain_ref, wx_ref, wfx_ref, slice_ref, heat_ref, cot_ref, wout_ref)
    copies = [pltpu.make_async_copy(a, b, sems.at[i]) for i, (a, b) in enumerate(zip(sources, targets))]
    for copy in copies:
        copy.start()
    valid = valid_column(rows_ref)
    ones = head_ones()
    copies[0].wait()
    xhat, rstd = normalise(x_ref[...])
    xhat_ref[...] = xhat
    rstd_ref[...] = rstd
    copies[1].wait()
    normed = (xhat * gain_ref[...]).astype(BF16)
    normed_ref[...] = normed
    copies[2].wait()
    mid = dot(normed, wx_ref[...]).astype(BF16)
    copies[3].wait()
    feat = dot(normed, wfx_ref[...]).astype(BF16)
    mid_ref[...] = mid
    feat_ref[...] = feat
    copies[4].wait()
    blocks = four_blocks(slice_ref[...])
    blocks_ref[...] = blocks
    copies[5].wait()
    heat = heat_ref[...]
    copies[6].wait()
    g_b = (cot_ref[...].astype(F32) * valid).astype(BF16)
    copies[7].wait()
    d_out = dot(g_b, wout_ref[...], ((1,), (1,))).astype(BF16)
    dout_ref[...] = d_out
    fold = fold_matrix()
    diagonal = (iota((256, 256), 0) >> 6) == ((iota((256, 256), 1) & 127) >> 5)
    tables, grads, masses = [], [], []
    for group in range(2):
        lanes = slice(group * 128, (group + 1) * 128)
        inv_temper = 1.0 / temper_row(heat, group)
        scaled, weights = weights_of(mid[:, lanes], blocks, inv_temper, ones, valid)
        sw = weights.astype(BF16)
        wide = slice(group * 256, (group + 1) * 256)
        temper_ref[:, wide] = inv_temper
        scaled_ref[:, wide] = scaled
        weights_ref[:, wide] = weights
        sw_ref[:, wide] = sw
        both = jnp.concatenate([feat[:, lanes], d_out[:, lanes]], axis=1)
        full = jnp.where(diagonal, dot(sw, both, ((0,), (0,))), 0.0).astype(BF16)
        tables.append(pack_rows(dot(full[:, :128], fold)))
        grads.append(pack_rows(dot(full[:, 128:], fold)))
        mass = jnp.sum(weights, axis=0, keepdims=True)
        for slab in range(2):
            pair = mass[:, slab * 128 : (slab + 1) * 128]
            masses += [pair, pltpu.roll(pair, 64, 1)]
    row = iota((8, 128), 0)
    mesh = mesh_ref[0]
    number = jnp.where(row == 1, ((mesh >> 1) + 1).astype(F32), 0.0)
    tails = [jnp.where(row == 0, mass, number)[None] for mass in masses]
    packed = [jnp.concatenate(tables, axis=0), jnp.concatenate(grads, axis=0), jnp.concatenate(tails, axis=0)]
    packed = jnp.concatenate(packed, axis=1)
    odd = (mesh & 1).astype(F32)
    both = jnp.concatenate([(packed * (1.0 - odd))[:, None], (packed * odd)[:, None]], axis=1)
    send_ref[...] = both.reshape(2 * HEADS, 40, 128).astype(BF16)


def dense_kernel(blocks_ref, out_ref):
    blocks = blocks_ref[...].astype(F32)
    numbers = blocks[:, 33:34, :]
    for k in range(OWNERS):
        out_ref[k] = jnp.sum(jnp.where(numbers == float(k + 1), blocks, 0.0), axis=0).astype(BF16)


def attend_kernel(sums_ref, qkv_ref, out_ref, grad_ref):
    sums = jnp.sum(sums_ref[...].astype(F32), axis=0)
    w_qkv = qkv_ref[...]
    eye = iota((SLICES, 128), 0) == iota((SLICES, 128), 1)
    mass = jnp.sum(jnp.where(eye, sums[32:33, :], 0.0), axis=1, keepdims=True)
    inv = 1.0 / (mass + EPS_MASS)

    def unfold(spread):
        return (spread[:, 0:32] + spread[:, 32:64]) + (spread[:, 64:96] + spread[:, 96:128])

    token = unfold(spread_rows(sums[None, 0:16, :])) * inv
    d_mixed = unfold(spread_rows(sums[None, 16:32, :])).astype(BF16).astype(F32)
    scale = 1.0 / math.sqrt(DH)
    query = dot(token, w_qkv[:, 0:32], precision=HIGHEST)
    keys = dot(token, w_qkv[:, 32:64], precision=HIGHEST)
    values = dot(token, w_qkv[:, 64:96], precision=HIGHEST)
    expo = jnp.exp(dot(query, keys, ((1,), (1,)), HIGHEST) * scale)
    probs = expo / jnp.sum(expo, axis=-1, keepdims=True)
    mixed = dot(probs, values, precision=HIGHEST)
    d_values = dot(probs, d_mixed, ((0,), (0,)), HIGHEST)
    d_probs = dot(d_mixed, values, ((1,), (1,)), HIGHEST)
    d_scores = probs * (d_probs - jnp.sum(probs * d_probs, axis=-1, keepdims=True)) * scale
    d_query = dot(d_scores, keys, precision=HIGHEST)
    d_keys = dot(d_scores, query, ((0,), (0,)), HIGHEST)
    d_qkv = jnp.concatenate([d_query, d_keys, d_values], axis=1)
    grad = dot(token, d_qkv, ((0,), (0,)), HIGHEST)
    grad_ref[...] = jnp.concatenate([grad, jnp.zeros((DH, 32), F32)], axis=1)
    d_token = dot(d_qkv, w_qkv, ((1,), (1,)), HIGHEST)
    d_table = d_token * inv
    d_mass = -jnp.sum(d_token * token, axis=1, keepdims=True) * inv

    def pack(values):
        return pack_rows(jnp.concatenate([values] * 4, axis=1))[0]

    tail = jnp.sum(jnp.where(eye, d_mass, 0.0), axis=0, keepdims=True)
    tail = jnp.where(iota((8, 128), 0) == 0, tail, 0.0)
    packed = jnp.concatenate([pack(mixed), pack(d_table), tail], axis=0).astype(BF16)
    out_ref[...] = jnp.broadcast_to(packed[None], (OWNERS, 40, 128))


def choose_kernel(blocks_ref, meshes_ref, out_ref):
    numbers = blocks_ref[...].astype(F32)[:, 33:34, :]
    meshes = meshes_ref[...].astype(F32)
    for b in range(2 * HEADS):
        chosen = jnp.zeros((40, 128), F32)
        for k in range(OWNERS):
            chosen = jnp.where(numbers[b] == float(k + 1), meshes[k], chosen)
        out_ref[b] = chosen.astype(BF16)


def back_kernel(
    rows_ref,
    normed_ref, mid_ref, feat_ref, sw_ref, dout_ref, scaled_ref, weights_ref, xhat_ref, rstd_ref,
    gain_ref, wx_ref, wfx_ref, cot_ref, blocks_ref, temper_ref, tokens_ref, qkv_grad_ref,
    feats_ref, mine_ref, other_ref,
):
    valid = valid_column(rows_ref)
    tokens = jnp.sum(tokens_ref[...].astype(F32).reshape(HEADS, 2, 40, 128), axis=1)
    blocks = blocks_ref[...]
    ones = head_ones()
    fold = fold_matrix()
    diagonal = (iota((256, 128), 0) >> 6) == (iota((256, 128), 1) >> 5)
    low_half = iota((1, 128), 1) < 64
    mid = mid_ref[...]
    feat = feat_ref[...]
    d_out = dout_ref[...]
    outs, d_mids, d_feats, slabs, temper_rows = [], [], [], [], []

    def block_of(packed):
        tiled = dot(spread_rows(packed).astype(BF16), fold)
        return jnp.where(diagonal, tiled, 0.0).astype(BF16)

    for group in range(2):
        lanes = slice(group * 128, (group + 1) * 128)
        heads = tokens[4 * group : 4 * group + 4]
        chosen = jnp.concatenate([block_of(heads[:, 0:16]), block_of(heads[:, 16:32])], axis=1)
        d_mass = [heads[i, 32:33, :] for i in range(4)]
        d_mass = jnp.concatenate(
            [jnp.where(low_half, d_mass[i], pltpu.roll(d_mass[i + 1], 64, 1)) for i in (0, 2)], axis=1
        )
        wide = slice(group * 256, (group + 1) * 256)
        sw = sw_ref[:, wide]
        pair = dot(sw, chosen)
        outs.append(pair[:, :128].astype(BF16))
        d_feats.append(pair[:, 128:].astype(BF16))
        left = jnp.concatenate([d_out[:, lanes], feat[:, lanes]], axis=1)
        d_sw = dot(left, chosen, ((1,), (1,))).astype(BF16).astype(F32)
        d_weights = d_sw + d_mass
        inv_temper = temper_ref[:, wide]
        scaled = scaled_ref[:, wide]
        weights = weights_ref[:, wide]
        d_scaled = weights * (d_weights - head_sums(weights * d_weights, ones))
        temper_rows.append(-jnp.sum(d_scaled * scaled, axis=0, keepdims=True) * inv_temper)
        d_logits = (d_scaled * inv_temper).astype(BF16)
        d_block = dot(mid[:, lanes], d_logits, ((0,), (0,)))
        for i in range(4):
            slabs.append(d_block[i * 32 : (i + 1) * 32, (i // 2) * 128 : (i // 2 + 1) * 128])
        d_mids.append(dot(d_logits, blocks, ((1,), (1,))).astype(BF16))
    slice_grad = jnp.where(
        low_half, (slabs[0] + slabs[2]) + (slabs[4] + slabs[6]), (slabs[1] + slabs[3]) + (slabs[5] + slabs[7])
    )
    d_mid = jnp.concatenate(d_mids, axis=1)
    d_feat = jnp.concatenate(d_feats, axis=1)
    g = cot_ref[...].astype(F32) * valid
    out_grad = dot(jnp.concatenate(outs, axis=1), g.astype(BF16), ((0,), (0,)))
    in_grads = dot(normed_ref[...], jnp.concatenate([d_mid, d_feat], axis=1), ((0,), (0,)))
    d_normed = dot(d_mid, wx_ref[...], ((1,), (1,))) + dot(d_feat, wfx_ref[...], ((1,), (1,)))
    d_normed = d_normed.astype(BF16).astype(F32)
    xhat = xhat_ref[...]
    gain_grad = jnp.sum(d_normed * xhat, axis=0, keepdims=True)
    d_xhat = d_normed * gain_ref[...]
    d_x = rstd_ref[...] * (
        d_xhat
        - jnp.mean(d_xhat, axis=-1, keepdims=True)
        - xhat * jnp.mean(d_xhat * xhat, axis=-1, keepdims=True)
    )
    feats_ref[...] = (g + d_x).astype(BF16)

    temper_grad = jnp.zeros((1, 128), F32)
    lane = iota((1, 128), 1)
    for group in range(2):
        head = iota((1, 256), 1) >> 6
        for i in range(4):
            total = jnp.sum(jnp.where(head == i, temper_rows[group], 0.0), axis=1, keepdims=True)
            temper_grad = jnp.where(lane == 4 * group + i, total, temper_grad)
    row = iota((8, 128), 0)
    vectors = jnp.where(row == 0, gain_grad[:, :128], jnp.where(row == 1, gain_grad[:, 128:], 0.0))
    vectors = jnp.where(row == 2, temper_grad, vectors)
    small = jnp.concatenate([slice_grad, qkv_grad_ref[...], vectors, jnp.zeros((184, 128), F32)], axis=0)
    halves = []
    for lanes, last in ((slice(0, 128), small), (slice(128, 256), jnp.zeros((WIDTH, 128), F32))):
        pieces = [out_grad[:, lanes], in_grads[:, :256][:, lanes], in_grads[:, 256:][:, lanes], last]
        halves.append(jnp.concatenate([piece.reshape(PEERS, SHARE, 128) for piece in pieces], axis=1))
    first = lax.axis_index("c") == 0
    mine_ref[...] = jnp.where(first, halves[0], halves[1]).astype(BF16)
    other_ref[...] = jnp.where(first, halves[1], halves[0]).astype(BF16)


def add_kernel(a_ref, b_ref, out_ref):
    out_ref[...] = (a_ref[...].astype(F32) + b_ref[...].astype(F32)).astype(BF16)


def sum_kernel(parts_ref, out_ref):
    total = jnp.sum(parts_ref[...].astype(F32), axis=0).astype(BF16)
    out_ref[...] = jnp.broadcast_to(total[None], out_ref.shape)


def finish_kernel(parts_ref, gain_ref, in_x_ref, in_fx_ref, slice_ref, temper_ref, qkv_ref, out_ref):
    parts = parts_ref[...].astype(F32)
    for at, ref in enumerate((out_ref, in_x_ref, in_fx_ref)):
        for half in range(2):
            piece = parts[half * PEERS : (half + 1) * PEERS, at * SHARE : (at + 1) * SHARE]
            ref[:, half * 128 : (half + 1) * 128] = piece.reshape(WIDTH, 128)
    small = parts[:PEERS, 3 * SHARE :].reshape(WIDTH, 128)
    slices = small[0:32]
    slice_ref[...] = slices[:, :64] + slices[:, 64:]
    qkv_ref[...] = small[32:64, :96]
    gain_ref[:, :128] = small[64:65]
    gain_ref[:, 128:] = small[65:66]
    temper_ref[...] = small[66:67, :8]


def call(kernel, name, inputs, outputs, scalars=0, far=False, scratch=()):
    specs = [pl.BlockSpec(memory_space=pltpu.SMEM)] * scalars
    specs += [pl.BlockSpec(memory_space=pltpu.HBM if far else pltpu.VMEM)] * (len(inputs) - scalars)
    single = not isinstance(outputs, (list, tuple))
    out_specs = pl.BlockSpec(memory_space=pltpu.VMEM)
    return pl.pallas_call(
        kernel,
        name=name,
        out_shape=outputs,
        in_specs=specs,
        out_specs=out_specs if single else [out_specs] * len(outputs),
        scratch_shapes=scratch,
        compiler_params=pltpu.CompilerParams(vmem_limit_bytes=48 * 1024 * 1024),
    )(*inputs)


def shape(dims, dtype=BF16):
    return jax.ShapeDtypeStruct(dims, dtype)


def shards(
    node_feats, cotangent, mesh_of_block, block_rows, ln_gain, w_in_x, w_in_fx, w_slice, temper, w_qkv, w_out
):
    x = node_feats.reshape(ROWS, WIDTH)
    cot = cotangent.reshape(ROWS, WIDTH)
    rows = block_rows.reshape(1)
    number = mesh_of_block.reshape(1)
    gain = ln_gain.reshape(1, WIDTH)
    wide = shape((ROWS, WIDTH))
    packets = shape((2 * HEADS, 40, 128))
    owned = shape((OWNERS, 40, 128))
    tall = shape((ROWS, 2 * WIDTH), F32)
    inputs = (x, gain, w_in_x, w_in_fx, w_slice, temper.reshape(1, HEADS), cot, w_out)
    far = [pltpu.with_memory_space_constraint(a, pltpu.HBM) for a in inputs]
    send, *kept = call(
        front_kernel,
        "front",
        (rows, number, *far),
        [
            packets, wide, wide, wide, shape((ROWS, 2 * WIDTH)), wide,
            tall, tall, shape((ROWS, WIDTH), F32), shape((ROWS, 1), F32),
            shape((1, WIDTH), F32), shape((WIDTH, WIDTH)), shape((WIDTH, WIDTH)), wide,
            shape((128, 256)), shape((1, 2 * WIDTH), F32),
        ],
        scalars=2,
        far=True,
        scratch=[pltpu.VMEM(inputs[i].shape, inputs[i].dtype) for i in (0, 4, 5, 7)]
        + [pltpu.SemaphoreType.DMA((len(far),))],
    )
    blocks = lax.all_to_all(send, ("y", "c", "zl"), 0, 0)
    dense = call(dense_kernel, "dense", (blocks,), owned)
    sums = lax.all_to_all(dense, "zh", 0, 0)
    answer, qkv_grad = call(attend_kernel, "attend", (sums, w_qkv), [owned, shape((DH, 128), F32)])
    meshes = lax.all_to_all(answer, "zh", 0, 0)
    chosen = call(choose_kernel, "choose", (blocks, meshes), packets)
    tokens = lax.all_to_all(chosen, ("y", "c", "zl"), 0, 0)
    share = shape((PEERS, 4 * SHARE, 128))
    feats_grad, mine, other = call(
        back_kernel, "back", (rows, *kept, tokens, qkv_grad), [wide, share, share], scalars=1
    )
    across = ("y", "zl", "x")
    other = lax.ppermute(other, "c", [(0, 1), (1, 0)])
    parts = call(add_kernel, "add_pair", (mine, other), share)
    parts = lax.all_to_all(parts, across, 0, 0)
    parts = call(sum_kernel, "sum_peers", (parts,), shape((OWNERS, 4 * SHARE, 128)))
    parts = lax.all_to_all(parts, "zh", 0, 0)
    parts = call(sum_kernel, "sum_z", (parts,), share)
    parts = lax.all_to_all(parts, across, 0, 0)
    parts = lax.all_gather(parts, "c", axis=0, tiled=True)
    square = shape((WIDTH, WIDTH), F32)
    gain_grad, in_x_grad, in_fx_grad, slice_grad, temper_grad, qkv_grad, out_grad = call(
        finish_kernel,
        "finish",
        (parts,),
        [
            shape((1, WIDTH), F32), square, square, shape((DH, SLICES), F32),
            shape((1, HEADS), F32), shape((DH, 3 * DH), F32), square,
        ],
    )
    return (
        feats_grad.reshape(1, 1, ROWS, WIDTH),
        gain_grad.reshape(WIDTH),
        in_x_grad,
        in_fx_grad,
        slice_grad,
        temper_grad.reshape(HEADS),
        qkv_grad,
        out_grad,
    )


def solution(mesh):
    groups = mesh.shape["dp"]
    devices = mesh.devices.reshape(4, OWNERS, 2, 2, groups)
    grid = Mesh(devices, ("y", "zh", "zl", "c", "x"))
    node = ("y", "zh", "zl", "c")
    blocks = P("x", node, None, None)
    scalars = P("x", node)
    return jax.shard_map(
        shards,
        mesh=grid,
        in_specs=(blocks, blocks, scalars, scalars) + (P(),) * 7,
        out_specs=(blocks,) + (P(),) * 7,
        check_vma=False,
    )
```

time: 1150 us -> 130 us (0.11)
  blocking collectives: 628 us -> 114 us
  waiting for transfers between devices: 344 us -> 1.14 us
  matrix products: 84.9 us -> 0 us
  local copies, waits for them, and re-layouts: 45.6 us -> 0.01 us
  other arithmetic: 24.8 us -> 0 us
  between operations: 16.4 us -> 1.98 us
    psum x2 -> x0, blocking collectives: 628 us -> none  [the longest x1 523 us: shards(): full_table, full_mass = lax.psum((table, mass), 'node')]
    psum x2 -> x0, waiting for transfers between devices: 344 us -> none  [the longest x1 344 us: shards(): lax.psum((gain_grad, in_x_grad, in_fx_grad, slice_grad, temper_grad, qkv_...]
    all_to_all x0 -> x7, blocking collectives: none -> 108 us  [the longest x2 25.4 us: shards(): parts = lax.all_to_all(parts, across, 0, 0)]
    dot_general x28 -> x0, matrix products: 84.9 us -> none  [the longest x3 24.1 us: attend(): jnp.einsum('pmd,pnd->pmn', query, keys, precision=lax.Precision.HIGHEST)]
    slice x4 -> x0, local copies, waits for them, and re-layouts: 13.9 us -> none  [the longest x2 5.79 us: attend(): query = qkv[..., :width]]
    unnamed x77 -> x2, local copies, waits for them, and re-layouts: 12.4 us -> 0.01 us
  transfers between devices with their start and end apart: 2 -> 1, of which waited for: 1 -> 1; matrix products, arithmetic and copies ran while one was open for 2% -> 0% of each run, Pallas kernels for 0% -> 0%
where the time goes in v1:
time: 130 us; the launch traced here: 129 us
  blocking collectives  114 us (88%)
  Pallas kernels  10.1 us (8%)
  starting transfers between devices  2.29 us (2%)
  between operations  1.98 us (2%)
    all_to_all x2, blocking collectives, shards(): parts = lax.all_to_all(parts, across, 0, 0)  25.4 us
    all_to_all x1, blocking collectives, shards(): sums = lax.all_to_all(dense, 'zh', 0, 0)  23.8 us
    all_to_all x1, blocking collectives, shards(): blocks = lax.all_to_all(send, ('y', 'c', 'zl'), 0, 0)  15.9 us
    all_to_all x1, blocking collectives, shards(): meshes = lax.all_to_all(answer, 'zh', 0, 0)  15.6 us
    all_to_all x1, blocking collectives, shards(): parts = lax.all_to_all(parts, 'zh', 0, 0)  14.6 us
    all_to_all x1, blocking collectives, shards(): tokens = lax.all_to_all(chosen, ('y', 'c', 'zl'), 0, 0)  12.7 us
    pallas_call x9, Pallas kernels, call(): pl.pallas_call(kernel, name=name, out_shape=outputs, in_specs=specs, out_...  10.1 us
    all_gather x1, blocking collectives, shards(): parts = lax.all_gather(parts, 'c', axis=0, tiled=True)  5.84 us
  transfers between devices with their start and end apart: 1, of which 1 were waited for; matrix products, arithmetic and copies ran while one was open for 0% of the time, Pallas kernels for 0%

profile of v1, /device:TPU:1, one launch (start us, length us, event | category | flops | bytes accessed | tf_op | source)
XLA Modules:
  0.0 129.3 jit_solution(3774456433890949431)
XLA Ops:
  1.9 3.8 %front.1 = (bf16[16,40,128]{2,1,0:T(8,128)(2,1)S(1)}, bf16[512,256]{1,0:T(8,128)(2,1)S(1)}, bf16[512,256]{1,0:T(8,128)(2,1)S(1)}, bf16[512,256]{1,0:T(8,128)(2,1...) custom-call(s32[1]{0:T(128)} %bitcast.10.rows_ref, ...), custom_call_target="tpu_custom_call" | custom-call | tf_op jit(solution)/shard_map/front/pallas_call | solution.py:342
  5.8 15.9 %all_to_all.35.blocks_ref = bf16[16,40,128]{2,1,0:T(8,128)(2,1)S(1)} all-to-all(bf16[16,40,128]{2,1,0:T(8,128)(2,1)S(1)} %get-tuple-element.51), channel_id=1, replica_groups=mesh['y'=4,'zh'=8,'zl'=2,'c'=2,'x'=4] {'y','c','zl'}, dimensions={0} | all-to-all | bytes 327680 | tf_op jit(solution)/shard_map/all_to_all | solution.py:386
  21.6 0.3 dense.1
  21.9 0.0 copy-start
  21.9 23.8 %all_to_all.36.sums_ref = bf16[8,40,128]{2,1,0:T(8,128)(2,1)S(1)} all-to-all(bf16[8,40,128]{2,1,0:T(8,128)(2,1)S(1)} %dense.1), channel_id=1, replica_groups=mesh['y'=4,'zh'=8,'zl'=2,'c'=2,'x'=4] {'zh'}, dimensions={0} | all-to-all | bytes 163840 | tf_op jit(solution)/shard_map/all_to_all | solution.py:388
  45.7 0.0 copy-done
  45.7 1.5 %attend.1 = (bf16[8,40,128]{2,1,0:T(8,128)(2,1)S(1)}, f32[32,128]{1,0:T(8,128)S(1)}) custom-call(bf16[8,40,128]{2,1,0:T(8,128)(2,1)S(1)} %all_to_all.36.sums_ref, f32[32,96]{1,0:T(8,128)S(1)} %copy-done), custom_call_target="tpu_custom_call" | custom-call | tf_op jit(solution)/shard_map/attend/pallas_call | solution.py:342
  47.2 15.6 %all_to_all.37.meshes_ref = bf16[8,40,128]{2,1,0:T(8,128)(2,1)S(1)} all-to-all(bf16[8,40,128]{2,1,0:T(8,128)(2,1)S(1)} %get-tuple-element.52), channel_id=1, replica_groups=mesh['y'=4,'zh'=8,'zl'=2,'c'=2,'x'=4] {'zh'}, dimensions={0} | all-to-all | bytes 163840 | tf_op jit(solution)/shard_map/all_to_all | solution.py:390
  62.8 0.2 choose.1
  62.9 12.7 %all_to_all.38.tokens_ref = bf16[16,40,128]{2,1,0:T(8,128)(2,1)S(1)} all-to-all(bf16[16,40,128]{2,1,0:T(8,128)(2,1)S(1)} %choose.1), channel_id=1, replica_groups=mesh['y'=4,'zh'=8,'zl'=2,'c'=2,'x'=4] {'y','c','zl'}, dimensions={0} | all-to-all | bytes 327680 | tf_op jit(solution)/shard_map/all_to_all | solution.py:392
  75.6 3.3 %back.1 = (bf16[512,256]{1,0:T(8,128)(2,1)}, bf16[32,32,128]{2,1,0:T(8,128)(2,1)S(1)}, bf16[32,32,128]{2,1,0:T(8,128)(2,1)S(1)}) custom-call(s32[1]{0:T(128)} %bitcast.11.rows_ref, bf16[512,256]{1,0:T(8,128)(2,1)S(1)} %get-tuple-element.36.normed_ref, bf16[512,256]{1,0:T(8,128)(2,1)S(1)} %get-tuple-element.37.mid_ref, ...), custom_call_target="tpu_custom_call" | custom-call | tf_op jit(solution)/shard_map/back/pallas_call | solution.py:342
  79.0 2.3 %collective-permute-start = (bf16[32,32,128]{2,1,0:T(8,128)(2,1)S(1)}, bf16[32,32,128]{2,1,0:T(8,128)(2,1)S(1)}, u32[]{:S(2)}, u32[]{:S(2)}) collective-permute-start(bf16[32,32,128]{2,1,0:T(8,128)(2,1)S(1)} %get-tuple-element.56), channel_id=1, source_target_pairs={{0,4},{4,0},{1,5},{5,1},{2,6},{6,2},{3,7},{7,3},{8,12},{12,8},{9,1... | collective-permute-start | bytes 786440 | tf_op jit(solution)/shard_map/ppermute | solution.py:398
  81.3 1.1 collective-permute-done.b_ref
  82.4 0.1 add_pair.1
  82.5 13.2 %all_to_all.39.parts_ref = bf16[32,32,128]{2,1,0:T(8,128)(2,1)S(1)} all-to-all(bf16[32,32,128]{2,1,0:T(8,128)(2,1)S(1)} %add_pair.1), channel_id=1, replica_groups=mesh['y'=4,'zh'=8,'zl'=2,'c'=2,'x'=4] {'y','zl','x'}, dimensions={0} | all-to-all | bytes 524288 | tf_op jit(solution)/shard_map/all_to_all | solution.py:400
  95.7 14.6 %all_to_all.40.parts_ref = bf16[8,32,128]{2,1,0:T(8,128)(2,1)S(1)} all-to-all(bf16[8,32,128]{2,1,0:T(8,128)(2,1)S(1)} %sum_peers.1), channel_id=1, replica_groups=mesh['y'=4,'zh'=8,'zl'=2,'c'=2,'x'=4] {'zh'}, dimensions={0} | all-to-all | bytes 131072 | tf_op jit(solution)/shard_map/all_to_all | solution.py:402
  110.3 12.2 %all_to_all.41 = bf16[32,32,128]{2,1,0:T(8,128)(2,1)S(1)} all-to-all(bf16[32,32,128]{2,1,0:T(8,128)(2,1)S(1)} %sum_z.1), channel_id=1, replica_groups=mesh['y'=4,'zh'=8,'zl'=2,'c'=2,'x'=4] {'y','zl','x'}, dimensions={0} | all-to-all | bytes 524288 | tf_op jit(solution)/shard_map/all_to_all | solution.py:404
  122.5 5.8 %all_gather.3.parts_ref = bf16[64,32,128]{2,1,0:T(8,128)(2,1)S(1)} all-gather(bf16[32,32,128]{2,1,0:T(8,128)(2,1)S(1)} %all_to_all.41), channel_id=1, replica_groups=mesh['y'=4,'zh'=8,'zl'=2,'c'=2,'x'=4] {'c'}, dimensions={0}, use_global_device_ids=true | all-gather | bytes 786432 | tf_op jit(solution)/shard_map/all_gather | solution.py:405
  128.4 0.9 finish.1
  (2 shorter events, 0.1 us)
Async XLA Ops:
  21.9 23.8 %copy-start = (f32[32,96]{1,0:T(8,128)S(1)}, f32[32,96]{1,0:T(8,128)}, u32[]{:S(2)}) copy-start(f32[32,96]{1,0:T(8,128)} %qkv_ref.1) | copy-start | bytes 36868
  79.0 3.4 %collective-permute-start = (bf16[32,32,128]{2,1,0:T(8,128)(2,1)S(1)}, bf16[32,32,128]{2,1,0:T(8,128)(2,1)S(1)}, u32[]{:S(2)}, u32[]{:S(2)}) collective-permute-start(bf16[32,32,128]{2,1,0:T(8,128)(2,1)S(1)} %get-tuple-element.56), channel_id=1, source_target_pairs={{0,4},{4,0},{1,5},{5,1},{2,6},{6,2},{3,7},{7,3},{8,12},{12,8},{9,1... | collective-permute-start | bytes 786440 | tf_op jit(solution)/shard_map/ppermute | solution.py:398

commit v2 on v1

v2 whole, which is shorter than its diff:
```python
import math

import jax
import jax.numpy as jnp
from jax import lax
from jax.experimental import pallas as pl
from jax.experimental.pallas import tpu as pltpu
from jax.sharding import Mesh
from jax.sharding import PartitionSpec as P

EPS_NORM = 1e-05
EPS_MASS = 1e-05
HEADS = 8
DH = 32
SLICES = 64
WIDTH = 256
ROWS = 512
OWNERS = 8
PEERS = 32
SHARE = 8
F32 = jnp.float32
BF16 = jnp.bfloat16
HIGHEST = lax.Precision.HIGHEST


def iota(shape, dim):
    return lax.broadcasted_iota(jnp.int32, shape, dim)


def dot(a, b, dims=((1,), (0,)), precision=None):
    return lax.dot_general(a, b, (dims, ((), ())), precision=precision, preferred_element_type=F32)


def four_blocks(w_slice):
    two = jnp.concatenate([w_slice, w_slice], axis=1)
    four = jnp.concatenate([two, two], axis=1)
    tall = jnp.concatenate([four] * 4, axis=0)
    same = (iota((128, 256), 0) >> 5) == (iota((128, 256), 1) >> 6)
    return jnp.where(same, tall, 0.0).astype(BF16)


def fold_matrix():
    return ((iota((128, 128), 0) & 31) == (iota((128, 128), 1) & 31)).astype(F32).astype(BF16)


def quarter_mask(rows):
    return ((iota((rows, 128), 0) & 63) >> 4) == (iota((rows, 128), 1) >> 5)


def pack_rows(tiled):
    rows = tiled.shape[0]
    kept = jnp.where(quarter_mask(rows), tiled, 0.0)
    return jnp.sum(kept.reshape(rows // 64, 4, 16, 128), axis=1)


def spread_rows(packed):
    heads = packed.shape[0]
    tall = jnp.broadcast_to(packed[:, None], (heads, 4, 16, 128)).reshape(heads * 64, 128)
    return jnp.where(quarter_mask(heads * 64), tall, 0.0)


def temper_column(temper, group):
    head = iota((256, 1), 0) >> 6
    column = jnp.zeros((256, 1), F32)
    for i in range(4):
        column = jnp.where(head == i, temper[:, 4 * group + i : 4 * group + i + 1], column)
    return column


def head_sums(values):
    rows, nodes = values.shape
    sums = jnp.sum(values.reshape(rows // 64, 64, nodes), axis=1, keepdims=True)
    return jnp.broadcast_to(sums, (rows // 64, 64, nodes)).reshape(rows, nodes)


def eye_mask():
    return iota((SLICES, 128), 0) == iota((SLICES, 128), 1)


def column_to_row(column):
    return jnp.sum(jnp.where(eye_mask(), column, 0.0), axis=0, keepdims=True)


def row_to_column(row):
    return jnp.sum(jnp.where(eye_mask(), row, 0.0), axis=1, keepdims=True)


def normalise(x):
    xf = x.astype(F32)
    mean = jnp.mean(xf, axis=-1, keepdims=True)
    centered = xf - mean
    var = jnp.mean(centered * centered, axis=-1, keepdims=True)
    rstd = lax.rsqrt(var + EPS_NORM)
    return centered * rstd, rstd


def front_kernel(
    rows_ref, mesh_ref, x_hbm, gain_hbm, wx_hbm, wfx_hbm, slice_hbm, temper_hbm, cot_hbm, wout_hbm,
    send_ref, normed_ref, mid_ref, feat_ref, sw_ref, dout_ref, scaled_ref, weights_ref, xhat_ref, rstd_ref,
    gain_ref, wx_ref, wfx_ref, g_ref, blocks_ref, temper_ref,
    x_ref, slice_ref, heat_ref, cot_ref, wout_ref, sems,
):
    sources = (x_hbm, gain_hbm, wx_hbm, wfx_hbm, slice_hbm, temper_hbm, cot_hbm, wout_hbm)
    targets = (x_ref, gain_ref, wx_ref, wfx_ref, slice_ref, heat_ref, cot_ref, wout_ref)
    copies = [pltpu.make_async_copy(a, b, sems.at[i]) for i, (a, b) in enumerate(zip(sources, targets))]
    for copy in copies:
        copy.start()
    copies[0].wait()
    xhat, rstd = normalise(x_ref[...])
    xhat_ref[...] = xhat
    rstd_ref[...] = rstd
    copies[1].wait()
    normed = (xhat * gain_ref[...]).astype(BF16)
    normed_ref[...] = normed
    copies[2].wait()
    mid = dot(wx_ref[...], normed, ((0,), (1,))).astype(BF16)
    copies[3].wait()
    feat = dot(normed, wfx_ref[...]).astype(BF16)
    mid_ref[...] = mid
    feat_ref[...] = feat
    copies[4].wait()
    blocks = four_blocks(slice_ref[...])
    blocks_ref[...] = blocks
    copies[5].wait()
    heat = heat_ref[...]
    copies[6].wait()
    g_b = jnp.where(iota((ROWS, 1), 0) < rows_ref[0, 0], cot_ref[...].astype(F32), 0.0).astype(BF16)
    g_ref[...] = g_b
    copies[7].wait()
    d_out = dot(g_b, wout_ref[...], ((1,), (1,))).astype(BF16)
    dout_ref[...] = d_out
    fold = fold_matrix()
    diagonal = (iota((256, 256), 0) >> 6) == ((iota((256, 256), 1) & 127) >> 5)
    valid = (iota((1, ROWS), 1) < rows_ref[0, 0]).astype(F32)
    tables, grads, masses = [], [], []
    for group in range(2):
        lanes = slice(group * 128, (group + 1) * 128)
        wide = slice(group * 256, (group + 1) * 256)
        inv_temper = 1.0 / temper_column(heat, group)
        temper_ref[wide, :] = inv_temper
        scaled = dot(blocks, mid[lanes], ((0,), (0,))) * inv_temper
        expo = jnp.exp(scaled)
        weights = expo / head_sums(expo) * valid
        sw = weights.astype(BF16)
        scaled_ref[wide, :] = scaled
        weights_ref[wide, :] = weights
        sw_ref[wide, :] = sw
        both = jnp.concatenate([feat[:, lanes], d_out[:, lanes]], axis=1)
        full = jnp.where(diagonal, dot(sw, both), 0.0).astype(BF16)
        tables.append(pack_rows(dot(full[:, :128], fold)))
        grads.append(pack_rows(dot(full[:, 128:], fold)))
        mass = jnp.sum(weights, axis=1, keepdims=True)
        masses += [column_to_row(mass[64 * i : 64 * i + 64]) for i in range(4)]
    row = iota((8, 128), 0)
    mesh = mesh_ref[0, 0]
    number = jnp.where(row == 1, ((mesh >> 1) + 1).astype(F32), 0.0)
    tails = [jnp.where(row == 0, mass, number)[None] for mass in masses]
    packed = [jnp.concatenate(tables, axis=0), jnp.concatenate(grads, axis=0), jnp.concatenate(tails, axis=0)]
    packed = jnp.concatenate(packed, axis=1)
    odd = (mesh & 1).astype(F32)
    both = jnp.concatenate([(packed * (1.0 - odd))[:, None], (packed * odd)[:, None]], axis=1)
    send_ref[...] = both.reshape(2 * HEADS, 40, 128).astype(BF16)


def dense_kernel(blocks_ref, out_ref):
    blocks = blocks_ref[...].astype(F32)
    numbers = blocks[:, 33:34, :]
    for k in range(OWNERS):
        out_ref[k] = jnp.sum(jnp.where(numbers == float(k + 1), blocks, 0.0), axis=0).astype(BF16)


def attend_kernel(sums_ref, qkv_ref, out_ref, token_ref, d_qkv_ref):
    sums = jnp.sum(sums_ref[...].astype(F32), axis=0)
    w_qkv = qkv_ref[...]
    mass = row_to_column(sums[32:33, :])
    inv = 1.0 / (mass + EPS_MASS)

    def unfold(spread):
        return (spread[:, 0:32] + spread[:, 32:64]) + (spread[:, 64:96] + spread[:, 96:128])

    token = unfold(spread_rows(sums[None, 0:16, :])) * inv
    d_mixed = unfold(spread_rows(sums[None, 16:32, :])).astype(BF16).astype(F32)
    scale = 1.0 / math.sqrt(DH)
    query = dot(token, w_qkv[:, 0:32], precision=HIGHEST)
    keys = dot(token, w_qkv[:, 32:64], precision=HIGHEST)
    values = dot(token, w_qkv[:, 64:96], precision=HIGHEST)
    expo = jnp.exp(dot(query, keys, ((1,), (1,)), HIGHEST) * scale)
    probs = expo / jnp.sum(expo, axis=-1, keepdims=True)
    mixed = dot(probs, values, precision=HIGHEST)
    d_values = dot(probs, d_mixed, ((0,), (0,)), HIGHEST)
    d_probs = dot(d_mixed, values, ((1,), (1,)), HIGHEST)
    d_scores = probs * (d_probs - jnp.sum(probs * d_probs, axis=-1, keepdims=True)) * scale
    d_query = dot(d_scores, keys, precision=HIGHEST)
    d_keys = dot(d_scores, query, ((0,), (0,)), HIGHEST)
    d_qkv = jnp.concatenate([d_query, d_keys, d_values], axis=1)
    token_ref[...] = token
    d_qkv_ref[...] = d_qkv
    d_token = dot(d_qkv, w_qkv, ((1,), (1,)), HIGHEST)
    d_table = d_token * inv
    d_mass = -jnp.sum(d_token * token, axis=1, keepdims=True) * inv

    def pack(values):
        return pack_rows(jnp.concatenate([values] * 4, axis=1))[0]

    tail = jnp.where(iota((8, 128), 0) == 0, column_to_row(d_mass), 0.0)
    packed = jnp.concatenate([pack(mixed), pack(d_table), tail], axis=0).astype(BF16)
    out_ref[...] = jnp.broadcast_to(packed[None], (OWNERS, 40, 128))


def choose_kernel(blocks_ref, meshes_ref, out_ref):
    numbers = blocks_ref[...].astype(F32)[:, 33:34, :]
    meshes = meshes_ref[...].astype(F32)
    for b in range(2 * HEADS):
        chosen = jnp.zeros((40, 128), F32)
        for k in range(OWNERS):
            chosen = jnp.where(numbers[b] == float(k + 1), meshes[k], chosen)
        out_ref[b] = chosen.astype(BF16)


def back_kernel(
    normed_ref, mid_ref, feat_ref, sw_ref, dout_ref, scaled_ref, weights_ref, g_ref, blocks_ref, temper_ref, tokens_ref,
    mine_ref, other_ref, dmid_ref, dfeat_ref, slice_ref, heat_ref,
):
    tokens = jnp.sum(tokens_ref[...].astype(F32).reshape(HEADS, 2, 40, 128), axis=1)
    blocks = blocks_ref[...]
    fold = fold_matrix()
    diagonal = (iota((256, 128), 0) >> 6) == (iota((256, 128), 1) >> 5)
    low_half = iota((1, 128), 1) < 64
    feat = feat_ref[...]
    d_out = dout_ref[...]
    outs, d_mids, d_feats, slabs = [], [], [], []
    temper_grad = jnp.zeros((1, 128), F32)
    lane = iota((1, 128), 1)

    def block_of(packed):
        tiled = dot(spread_rows(packed).astype(BF16), fold)
        return jnp.where(diagonal, tiled, 0.0).astype(BF16)

    for group in range(2):
        lanes = slice(group * 128, (group + 1) * 128)
        wide = slice(group * 256, (group + 1) * 256)
        heads = tokens[4 * group : 4 * group + 4]
        chosen = jnp.concatenate([block_of(heads[:, 0:16]), block_of(heads[:, 16:32])], axis=1)
        d_mass = jnp.concatenate([row_to_column(heads[i, 32:33, :]) for i in range(4)], axis=0)
        pair = dot(chosen, sw_ref[wide, :], ((0,), (0,)))
        outs.append(pair[:128].astype(BF16))
        d_feats.append(pair[128:].astype(BF16))
        left = jnp.concatenate([d_out[:, lanes], feat[:, lanes]], axis=1)
        d_sw = dot(chosen, left, ((1,), (1,))).astype(BF16).astype(F32)
        d_weights = d_sw + d_mass
        inv_temper = temper_ref[wide, :]
        weights = weights_ref[wide, :]
        d_scaled = weights * (d_weights - head_sums(weights * d_weights))
        products = jnp.sum((d_scaled * scaled_ref[wide, :]).reshape(4, SLICES, ROWS), axis=1)
        totals = jnp.sum(products, axis=1, keepdims=True)
        for i in range(4):
            total = -totals[i : i + 1] * inv_temper[64 * i : 64 * i + 1]
            temper_grad = jnp.where(lane == 4 * group + i, total, temper_grad)
        d_logits = (d_scaled * inv_temper).astype(BF16)
        d_block = dot(mid_ref[lanes, :], d_logits, ((1,), (1,)))
        for i in range(4):
            slabs.append(d_block[i * 32 : (i + 1) * 32, (i // 2) * 128 : (i // 2 + 1) * 128])
        d_mids.append(dot(blocks, d_logits).astype(BF16))
    heat_ref[...] = temper_grad
    slice_ref[...] = jnp.where(
        low_half, (slabs[0] + slabs[2]) + (slabs[4] + slabs[6]), (slabs[1] + slabs[3]) + (slabs[5] + slabs[7])
    )
    d_mid = jnp.concatenate(d_mids, axis=0)
    d_feat = jnp.concatenate(d_feats, axis=0)
    dmid_ref[...] = d_mid
    dfeat_ref[...] = d_feat
    out_grad = dot(jnp.concatenate(outs, axis=0), g_ref[...])
    in_grads = dot(normed_ref[...], jnp.concatenate([d_mid, d_feat], axis=0), ((0,), (1,)))
    halves = []
    for lanes in (slice(0, 128), slice(128, 256)):
        pieces = [out_grad[:, lanes], in_grads[:, :256][:, lanes], in_grads[:, 256:][:, lanes]]
        halves.append(jnp.concatenate([piece.reshape(PEERS, SHARE, 128) for piece in pieces], axis=1))
    first = lax.axis_index("c") == 0
    mine_ref[...] = jnp.where(first, halves[0], halves[1]).astype(BF16)
    other_ref[...] = jnp.where(first, halves[1], halves[0]).astype(BF16)


def norm_kernel(
    dmid_ref, dfeat_ref, wx_ref, wfx_ref, xhat_ref, rstd_ref, gain_ref, g_ref, slice_ref, heat_ref, token_ref, d_qkv_ref,
    feats_ref, small_ref,
):
    d_normed = dot(dmid_ref[...], wx_ref[...], ((0,), (1,))) + dot(dfeat_ref[...], wfx_ref[...], ((0,), (1,)))
    d_normed = d_normed.astype(BF16).astype(F32)
    xhat = xhat_ref[...]
    gain_grad = jnp.sum(d_normed * xhat, axis=0, keepdims=True)
    d_xhat = d_normed * gain_ref[...]
    d_x = rstd_ref[...] * (
        d_xhat
        - jnp.mean(d_xhat, axis=-1, keepdims=True)
        - xhat * jnp.mean(d_xhat * xhat, axis=-1, keepdims=True)
    )
    feats_ref[...] = (g_ref[...].astype(F32) + d_x).astype(BF16)
    qkv_grad = dot(token_ref[...], d_qkv_ref[...], ((0,), (0,)), HIGHEST)
    row = iota((8, 128), 0)
    vectors = jnp.where(row == 0, gain_grad[:, :128], jnp.where(row == 1, gain_grad[:, 128:], 0.0))
    small_ref[0:32, :] = slice_ref[...]
    small_ref[32:64, :] = jnp.concatenate([qkv_grad, jnp.zeros((DH, 32), F32)], axis=1)
    small_ref[64:72, :] = jnp.where(row == 2, heat_ref[...], vectors)
    small_ref[72:, :] = jnp.zeros((WIDTH - 72, 128), F32)


def add_kernel(a_ref, b_ref, small_ref, out_ref):
    total = a_ref[...].astype(F32) + b_ref[...].astype(F32)
    small = small_ref[...].reshape(PEERS, SHARE, 128)
    out_ref[...] = jnp.concatenate([total, small], axis=1).astype(BF16)


def sum_kernel(parts_ref, out_ref):
    total = jnp.sum(parts_ref[...].astype(F32), axis=0).astype(BF16)
    out_ref[...] = jnp.broadcast_to(total[None], out_ref.shape)


def finish_kernel(
    parts_ref,
    gain_hbm, in_x_hbm, in_fx_hbm, slice_hbm, temper_hbm, qkv_hbm, out_hbm,
    gain_ref, in_x_ref, in_fx_ref, slice_ref, temper_ref, qkv_ref, out_ref, sems,
):
    copies = []

    def leave(source, target):
        copies.append(pltpu.make_async_copy(source, target, sems.at[len(copies)]))
        copies[-1].start()

    for at, (ref, hbm) in enumerate(((out_ref, out_hbm), (in_x_ref, in_x_hbm), (in_fx_ref, in_fx_hbm))):
        for half in range(2):
            piece = parts_ref[half * PEERS : (half + 1) * PEERS].astype(F32)[:, at * SHARE : (at + 1) * SHARE]
            ref[:, half * 128 : (half + 1) * 128] = piece.reshape(WIDTH, 128)
        leave(ref, hbm)
    small = parts_ref[:PEERS].astype(F32)[:, 3 * SHARE :] + parts_ref[PEERS:].astype(F32)[:, 3 * SHARE :]
    small = small.reshape(WIDTH, 128)
    slices = small[0:32]
    slice_ref[...] = slices[:, :64] + slices[:, 64:]
    leave(slice_ref, slice_hbm)
    qkv_ref[...] = small[32:64, :96]
    leave(qkv_ref, qkv_hbm)
    gain_ref[:, :128] = small[64:65]
    gain_ref[:, 128:] = small[65:66]
    leave(gain_ref, gain_hbm)
    temper_ref[...] = small[66:67, :8]
    leave(temper_ref, temper_hbm)
    for copy in copies:
        copy.wait()


def call(kernel, name, inputs, outputs, scalars=0, far_in=False, far_out=False, scratch=(), cost=None):
    single = not isinstance(outputs, (list, tuple))
    in_spec = pl.BlockSpec(memory_space=pltpu.HBM if far_in else pltpu.VMEM)
    out_spec = pl.BlockSpec(memory_space=pltpu.HBM if far_out else pltpu.VMEM)
    return pl.pallas_call(
        kernel,
        name=name,
        out_shape=outputs,
        in_specs=[pl.BlockSpec(memory_space=pltpu.SMEM)] * scalars + [in_spec] * (len(inputs) - scalars),
        out_specs=out_spec if single else [out_spec] * len(outputs),
        scratch_shapes=scratch,
        compiler_params=pltpu.CompilerParams(vmem_limit_bytes=48 * 1024 * 1024),
        cost_estimate=cost,
    )(*inputs)


def shape(dims, dtype=BF16):
    return jax.ShapeDtypeStruct(dims, dtype)


def shards(
    node_feats, cotangent, mesh_of_block, block_rows, ln_gain, w_in_x, w_in_fx, w_slice, temper, w_qkv, w_out
):
    x = node_feats.reshape(ROWS, WIDTH)
    cot = cotangent.reshape(ROWS, WIDTH)
    gain = ln_gain.reshape(1, WIDTH)
    wide = shape((ROWS, WIDTH))
    packets = shape((2 * HEADS, 40, 128))
    owned = shape((OWNERS, 40, 128))
    tall = shape((2 * WIDTH, ROWS), F32)
    flat = shape((WIDTH, ROWS))
    inputs = (x, gain, w_in_x, w_in_fx, w_slice, temper.reshape(1, HEADS), cot, w_out)
    far = [pltpu.with_memory_space_constraint(a, pltpu.HBM) for a in inputs]
    scratch = [pltpu.VMEM(a.shape, a.dtype) for a in (x, w_slice, inputs[5], cot, w_out)]
    scratch.append(pltpu.SemaphoreType.DMA((len(far),)))
    send, normed, mid, feat, sw, d_out, scaled, weights, xhat, rstd, gains, wx, wfx, g, diagonal, heat = call(
        front_kernel,
        "front",
        (block_rows, mesh_of_block, *far),
        [
            packets, wide, flat, wide, shape((2 * WIDTH, ROWS)), wide,
            tall, tall, shape((ROWS, WIDTH), F32), shape((ROWS, 1), F32),
            shape((1, WIDTH), F32), shape((WIDTH, WIDTH)), shape((WIDTH, WIDTH)), wide,
            shape((128, 256)), shape((2 * WIDTH, 1), F32),
        ],
        scalars=2,
        far_in=True,
        scratch=scratch,
    )
    blocks = lax.all_to_all(send, ("y", "c", "zl"), 0, 0)
    dense = call(dense_kernel, "dense", (blocks,), owned)
    sums = lax.all_to_all(dense, "zh", 0, 0)
    answer, token, d_qkv = call(
        attend_kernel,
        "attend",
        (sums, w_qkv),
        [owned, shape((SLICES, DH), F32), shape((SLICES, 3 * DH), F32)],
    )
    meshes = lax.all_to_all(answer, "zh", 0, 0)
    chosen = call(choose_kernel, "choose", (blocks, meshes), packets)
    tokens = lax.all_to_all(chosen, ("y", "c", "zl"), 0, 0)
    share = shape((PEERS, 4 * SHARE, 128))
    big = shape((PEERS, 3 * SHARE, 128))
    mine, other, d_mid, d_feat, slice_grad, temper_grad = call(
        back_kernel,
        "back",
        (normed, mid, feat, sw, d_out, scaled, weights, g, diagonal, heat, tokens),
        [big, big, flat, flat, shape((DH, 128), F32), shape((1, 128), F32)],
    )
    other = lax.ppermute(other, "c", [(0, 1), (1, 0)])
    feats_grad, small = call(
        norm_kernel,
        "norm",
        (d_mid, d_feat, wx, wfx, xhat, rstd, gains, g, slice_grad, temper_grad, token, d_qkv),
        [wide, shape((WIDTH, 128), F32)],
        cost=pl.CostEstimate(flops=4 * ROWS * WIDTH * WIDTH, bytes_accessed=4 * 1024 * 1024, transcendentals=0),
    )
    across = ("y", "zl", "x")
    parts = call(add_kernel, "add_pair", (mine, other, small), share)
    parts = lax.all_to_all(parts, across, 0, 0)
    parts = call(sum_kernel, "sum_peers", (parts,), shape((OWNERS, 4 * SHARE, 128)))
    parts = lax.all_to_all(parts, "zh", 0, 0)
    parts = call(sum_kernel, "sum_z", (parts,), share)
    parts = lax.all_to_all(parts, across, 0, 0)
    parts = lax.all_gather(parts, "c", axis=0, tiled=True)
    square = shape((WIDTH, WIDTH), F32)
    results = [
        shape((1, WIDTH), F32), square, square, shape((DH, SLICES), F32),
        shape((1, HEADS), F32), shape((DH, 3 * DH), F32), square,
    ]
    gain_grad, in_x_grad, in_fx_grad, slice_grad, temper_grad, qkv_grad, out_grad = call(
        finish_kernel,
        "finish",
        (parts,),
        results,
        far_out=True,
        scratch=[pltpu.VMEM(r.shape, r.dtype) for r in results] + [pltpu.SemaphoreType.DMA((len(results),))],
    )
    return (
        feats_grad.reshape(1, 1, ROWS, WIDTH),
        gain_grad.reshape(WIDTH),
        in_x_grad,
        in_fx_grad,
        slice_grad,
        temper_grad.reshape(HEADS),
        qkv_grad,
        out_grad,
    )


def solution(mesh):
    groups = mesh.shape["dp"]
    devices = mesh.devices.reshape(4, OWNERS, 2, 2, groups)
    grid = Mesh(devices, ("y", "zh", "zl", "c", "x"))
    node = ("y", "zh", "zl", "c")
    blocks = P("x", node, None, None)
    scalars = P("x", node)
    return jax.shard_map(
        shards,
        mesh=grid,
        in_specs=(blocks, blocks, scalars, scalars) + (P(),) * 7,
        out_specs=(blocks,) + (P(),) * 7,
        check_vma=False,
    )
```

time: 130 us -> 128 us (0.985)
    pallas_call x9 -> x10, Pallas kernels: 10.1 us -> 9.51 us  [call(): pl.pallas_call(kernel, name=name, out_shape=outputs, in_specs=[pl.BlockSp...]
  transfers between devices with their start and end apart: 1 -> 1, of which waited for: 1 -> 0; matrix products, arithmetic and copies ran while one was open for 0% -> 0% of each run, Pallas kernels for 0% -> 1%
where the time goes in v2:
time: 128 us
  blocking collectives  114 us (89%)
  Pallas kernels  9.51 us (7%)
  starting transfers between devices  2.3 us (2%)
  between operations  1.98 us (2%)
    all_to_all x2, blocking collectives, shards(): parts = lax.all_to_all(parts, across, 0, 0)  25.4 us
    all_to_all x1, blocking collectives, shards(): sums = lax.all_to_all(dense, 'zh', 0, 0)  23.8 us
    all_to_all x1, blocking collectives, shards(): blocks = lax.all_to_all(send, ('y', 'c', 'zl'), 0, 0)  15.9 us
    all_to_all x1, blocking collectives, shards(): meshes = lax.all_to_all(answer, 'zh', 0, 0)  15.6 us
    all_to_all x1, blocking collectives, shards(): parts = lax.all_to_all(parts, 'zh', 0, 0)  14.6 us
    all_to_all x1, blocking collectives, shards(): tokens = lax.all_to_all(chosen, ('y', 'c', 'zl'), 0, 0)  12.7 us
    pallas_call x10, Pallas kernels, call(): pl.pallas_call(kernel, name=name, out_shape=outputs, in_specs=[pl.BlockSp...  9.51 us
    all_gather x1, blocking collectives, shards(): parts = lax.all_gather(parts, 'c', axis=0, tiled=True)  5.84 us
  transfers between devices with their start and end apart: 1, of which 0 were waited for; matrix products, arithmetic and copies ran while one was open for 0% of the time, Pallas kernels for 1%

profile of v2, /device:TPU:1, one launch (start us, length us, event | category | flops | bytes accessed | tf_op | source)
XLA Modules:
  0.0 127.5 jit_solution(8405366335356851171)
XLA Ops:
  1.9 3.3 %front.1 = (bf16[16,40,128]{2,1,0:T(8,128)(2,1)S(1)}, bf16[512,256]{1,0:T(8,128)(2,1)S(1)}, bf16[256,512]{1,0:T(8,128)(2,1)S(1)}, bf16[512,256]{1,0:T(8,128)(2,1...) custom-call(s32[1,1]{1,0:T(1,128)S(6)} %copy.20.rows_ref, ...), custom_call_target="tpu_custom_call" | custom-call | tf_op jit(solution)/shard_map/front/pallas_call | solution.py:354
  5.3 15.9 %all_to_all.35.blocks_ref = bf16[16,40,128]{2,1,0:T(8,128)(2,1)S(1)} all-to-all(bf16[16,40,128]{2,1,0:T(8,128)(2,1)S(1)} %get-tuple-element.52), channel_id=1, replica_groups=mesh['y'=4,'zh'=8,'zl'=2,'c'=2,'x'=4] {'y','c','zl'}, dimensions={0} | all-to-all | bytes 327680 | tf_op jit(solution)/shard_map/all_to_all | solution.py:399
  21.2 0.3 dense.1
  21.4 0.0 copy-start
  21.4 23.8 %all_to_all.36.sums_ref = bf16[8,40,128]{2,1,0:T(8,128)(2,1)S(1)} all-to-all(bf16[8,40,128]{2,1,0:T(8,128)(2,1)S(1)} %dense.1), channel_id=1, replica_groups=mesh['y'=4,'zh'=8,'zl'=2,'c'=2,'x'=4] {'zh'}, dimensions={0} | all-to-all | bytes 163840 | tf_op jit(solution)/shard_map/all_to_all | solution.py:401
  45.2 0.0 copy-done
  45.2 1.4 %attend.1 = (bf16[8,40,128]{2,1,0:T(8,128)(2,1)S(1)}, f32[64,32]{1,0:T(8,128)S(1)}, f32[64,96]{1,0:T(8,128)S(1)}) custom-call(bf16[8,40,128]{2,1,0:T(8,128)(2,1)S(1)} %all_to_all.36.sums_ref, f32[32,96]{1,0:T(8,128)S(1)} %copy-done), custom_call_target="tpu_custom_call" | custom-call | tf_op jit(solution)/shard_map/attend/pallas_call | solution.py:354
  46.6 15.6 %all_to_all.37.meshes_ref = bf16[8,40,128]{2,1,0:T(8,128)(2,1)S(1)} all-to-all(bf16[8,40,128]{2,1,0:T(8,128)(2,1)S(1)} %get-tuple-element.53), channel_id=1, replica_groups=mesh['y'=4,'zh'=8,'zl'=2,'c'=2,'x'=4] {'zh'}, dimensions={0} | all-to-all | bytes 163840 | tf_op jit(solution)/shard_map/all_to_all | solution.py:408
  62.1 0.2 choose.1
  62.3 12.7 %all_to_all.38.tokens_ref = bf16[16,40,128]{2,1,0:T(8,128)(2,1)S(1)} all-to-all(bf16[16,40,128]{2,1,0:T(8,128)(2,1)S(1)} %choose.1), channel_id=1, replica_groups=mesh['y'=4,'zh'=8,'zl'=2,'c'=2,'x'=4] {'y','c','zl'}, dimensions={0} | all-to-all | bytes 327680 | tf_op jit(solution)/shard_map/all_to_all | solution.py:410
  75.0 1.9 %back.1 = (bf16[32,24,128]{2,1,0:T(8,128)(2,1)S(1)}, bf16[32,24,128]{2,1,0:T(8,128)(2,1)S(1)}, bf16[256,512]{1,0:T(8,128)(2,1)S(1)}, bf16[256,512]{1,0:T(8,128)(...) custom-call(bf16[512,256]{1,0:T(8,128)(2,1)S(1)} %get-tuple-element.42.normed_ref, ...), custom_call_target="tpu_custom_call" | custom-call | tf_op jit(solution)/shard_map/back/pallas_call | solution.py:354
  76.9 2.3 %collective-permute-start = (bf16[32,24,128]{2,1,0:T(8,128)(2,1)S(1)}, bf16[32,24,128]{2,1,0:T(8,128)(2,1)S(1)}, u32[]{:S(2)}, u32[]{:S(2)}) collective-permute-start(bf16[32,24,128]{2,1,0:T(8,128)(2,1)S(1)} %get-tuple-element.67), channel_id=1, source_target_pairs={{0,4},{4,0},{1,5},{5,1},{2,6},{6,2},{3,7},{7,3},{8,12},{12,8},{9,1... | collective-permute-start | bytes 589832 | tf_op jit(solution)/shard_map/ppermute | solution.py:419
  79.3 1.4 %norm.1 = (bf16[512,256]{1,0:T(8,128)(2,1)}, f32[256,128]{1,0:T(8,128)S(1)}) custom-call(bf16[256,512]{1,0:T(8,128)(2,1)S(1)} %get-tuple-element.54.dmid_ref, bf16[256,512]{1,0:T(8,128)(2,1)S(1)} %get-tuple-element.55.dfeat_ref, bf16[256,256]{1,0:T(8,128)(2,1)S(1)} %get-tuple-element.56.wx_ref, bf16[256,256]{1,0:T(8,128)(2,1)S(1)} %get-tuple-element.57.wfx_ref, ...), custom_call_target="tpu_custom_call" | custom-call | flops 134217728 | bytes 4194304 | tf_op jit(solution)/shard_map/norm/pallas_call | solution.py:354
  80.6 0.0 collective-permute-done.b_ref
  80.6 0.1 add_pair.1
  80.7 13.2 %all_to_all.39.parts_ref = bf16[32,32,128]{2,1,0:T(8,128)(2,1)S(1)} all-to-all(bf16[32,32,128]{2,1,0:T(8,128)(2,1)S(1)} %add_pair.1), channel_id=1, replica_groups=mesh['y'=4,'zh'=8,'zl'=2,'c'=2,'x'=4] {'y','zl','x'}, dimensions={0} | all-to-all | bytes 524288 | tf_op jit(solution)/shard_map/all_to_all | solution.py:429
  93.9 14.6 %all_to_all.40.parts_ref = bf16[8,32,128]{2,1,0:T(8,128)(2,1)S(1)} all-to-all(bf16[8,32,128]{2,1,0:T(8,128)(2,1)S(1)} %sum_peers.1), channel_id=1, replica_groups=mesh['y'=4,'zh'=8,'zl'=2,'c'=2,'x'=4] {'zh'}, dimensions={0} | all-to-all | bytes 131072 | tf_op jit(solution)/shard_map/all_to_all | solution.py:431
  108.5 12.2 %all_to_all.41 = bf16[32,32,128]{2,1,0:T(8,128)(2,1)S(1)} all-to-all(bf16[32,32,128]{2,1,0:T(8,128)(2,1)S(1)} %sum_z.1), channel_id=1, replica_groups=mesh['y'=4,'zh'=8,'zl'=2,'c'=2,'x'=4] {'y','zl','x'}, dimensions={0} | all-to-all | bytes 524288 | tf_op jit(solution)/shard_map/all_to_all | solution.py:433
  120.7 5.8 %all_gather.3.parts_ref = bf16[64,32,128]{2,1,0:T(8,128)(2,1)S(1)} all-gather(bf16[32,32,128]{2,1,0:T(8,128)(2,1)S(1)} %all_to_all.41), channel_id=1, replica_groups=mesh['y'=4,'zh'=8,'zl'=2,'c'=2,'x'=4] {'c'}, dimensions={0}, use_global_device_ids=true | all-gather | bytes 786432 | tf_op jit(solution)/shard_map/all_gather | solution.py:434
  126.6 1.0 finish.1
  (2 shorter events, 0.1 us)
Async XLA Ops:
  21.4 23.8 %copy-start = (f32[32,96]{1,0:T(8,128)S(1)}, f32[32,96]{1,0:T(8,128)}, u32[]{:S(2)}) copy-start(f32[32,96]{1,0:T(8,128)} %qkv_ref.1) | copy-start | bytes 36868
  76.9 3.7 %collective-permute-start = (bf16[32,24,128]{2,1,0:T(8,128)(2,1)S(1)}, bf16[32,24,128]{2,1,0:T(8,128)(2,1)S(1)}, u32[]{:S(2)}, u32[]{:S(2)}) collective-permute-start(bf16[32,24,128]{2,1,0:T(8,128)(2,1)S(1)} %get-tuple-element.67), channel_id=1, source_target_pairs={{0,4},{4,0},{1,5},{5,1},{2,6},{6,2},{3,7},{7,3},{8,12},{12,8},{9,1... | collective-permute-start | bytes 589832 | tf_op jit(solution)/shard_map/ppermute | solution.py:419

commit v3 on v2

--- a/solution.py
+++ b/solution.py
@@ -158,8 +158,7 @@
     packed = [jnp.concatenate(tables, axis=0), jnp.concatenate(grads, axis=0), jnp.concatenate(tails, axis=0)]
     packed = jnp.concatenate(packed, axis=1)
     odd = (mesh & 1).astype(F32)
-    both = jnp.concatenate([(packed * (1.0 - odd))[:, None], (packed * odd)[:, None]], axis=1)
-    send_ref[...] = both.reshape(2 * HEADS, 40, 128).astype(BF16)
+    send_ref[...] = jnp.concatenate([packed * (1.0 - odd), packed * odd], axis=0).astype(BF16)
 
 
 def dense_kernel(blocks_ref, out_ref):
@@ -221,7 +220,7 @@
     normed_ref, mid_ref, feat_ref, sw_ref, dout_ref, scaled_ref, weights_ref, g_ref, blocks_ref, temper_ref, tokens_ref,
     mine_ref, other_ref, dmid_ref, dfeat_ref, slice_ref, heat_ref,
 ):
-    tokens = jnp.sum(tokens_ref[...].astype(F32).reshape(HEADS, 2, 40, 128), axis=1)
+    tokens = jnp.sum(tokens_ref[...].astype(F32).reshape(2, HEADS, 40, 128), axis=0)
     blocks = blocks_ref[...]
     fold = fold_matrix()
     diagonal = (iota((256, 128), 0) >> 6) == (iota((256, 128), 1) >> 5)
@@ -396,18 +395,18 @@
         far_in=True,
         scratch=scratch,
     )
-    blocks = lax.all_to_all(send, ("y", "c", "zl"), 0, 0)
+    blocks = lax.all_to_all(send, ("zl", "y", "c"), 0, 0)
     dense = call(dense_kernel, "dense", (blocks,), owned)
-    sums = lax.all_to_all(dense, "zh", 0, 0)
+    sums = lax.all_to_all(dense, ("zb", "zc", "za"), 0, 0)
     answer, token, d_qkv = call(
         attend_kernel,
         "attend",
         (sums, w_qkv),
         [owned, shape((SLICES, DH), F32), shape((SLICES, 3 * DH), F32)],
     )
-    meshes = lax.all_to_all(answer, "zh", 0, 0)
+    meshes = lax.all_to_all(answer, ("zb", "zc", "za"), 0, 0)
     chosen = call(choose_kernel, "choose", (blocks, meshes), packets)
-    tokens = lax.all_to_all(chosen, ("y", "c", "zl"), 0, 0)
+    tokens = lax.all_to_all(chosen, ("zl", "y", "c"), 0, 0)
     share = shape((PEERS, 4 * SHARE, 128))
     big = shape((PEERS, 3 * SHARE, 128))
     mine, other, d_mid, d_feat, slice_grad, temper_grad = call(
@@ -428,7 +427,7 @@
     parts = call(add_kernel, "add_pair", (mine, other, small), share)
     parts = lax.all_to_all(parts, across, 0, 0)
     parts = call(sum_kernel, "sum_peers", (parts,), shape((OWNERS, 4 * SHARE, 128)))
-    parts = lax.all_to_all(parts, "zh", 0, 0)
+    parts = lax.all_to_all(parts, ("zb", "zc", "za"), 0, 0)
     parts = call(sum_kernel, "sum_z", (parts,), share)
     parts = lax.all_to_all(parts, across, 0, 0)
     parts = lax.all_gather(parts, "c", axis=0, tiled=True)
@@ -459,9 +458,9 @@
 
 def solution(mesh):
     groups = mesh.shape["dp"]
-    devices = mesh.devices.reshape(4, OWNERS, 2, 2, groups)
-    grid = Mesh(devices, ("y", "zh", "zl", "c", "x"))
-    node = ("y", "zh", "zl", "c")
+    devices = mesh.devices.reshape(4, 2, 2, 2, 2, 2, groups)
+    grid = Mesh(devices, ("y", "za", "zb", "zc", "zl", "c", "x"))
+    node = ("y", "za", "zb", "zc", "zl", "c")
     blocks = P("x", node, None, None)
     scalars = P("x", node)
     return jax.shard_map(

time: 128 us -> 126 us (0.984)
  blocking collectives: 114 us -> 112 us
    all_to_all x5, blocking collectives: 82.5 us -> 80.7 us  [the longest x1 23 us: shards(): sums = lax.all_to_all(dense, ('zb', 'zc', 'za'), 0, 0)]
where the time goes in v3:
time: 126 us
  blocking collectives  112 us (89%)
  Pallas kernels  9.49 us (8%)
  starting transfers between devices  2.66 us (2%)
  between operations  1.98 us (2%)
    all_to_all x2, blocking collectives, shards(): parts = lax.all_to_all(parts, across, 0, 0)  25.2 us
    all_to_all x1, blocking collectives, shards(): sums = lax.all_to_all(dense, ('zb', 'zc', 'za'), 0, 0)  23 us
    all_to_all x1, blocking collectives, shards(): blocks = lax.all_to_all(send, ('zl', 'y', 'c'), 0, 0)  15.8 us
    all_to_all x1, blocking collectives, shards(): meshes = lax.all_to_all(answer, ('zb', 'zc', 'za'), 0, 0)  15.3 us
    all_to_all x1, blocking collectives, shards(): parts = lax.all_to_all(parts, ('zb', 'zc', 'za'), 0, 0)  14 us
    all_to_all x1, blocking collectives, shards(): tokens = lax.all_to_all(chosen, ('zl', 'y', 'c'), 0, 0)  12.6 us
    pallas_call x10, Pallas kernels, call(): pl.pallas_call(kernel, name=name, out_shape=outputs, in_specs=[pl.BlockSp...  9.49 us
    all_gather x1, blocking collectives, shards(): parts = lax.all_gather(parts, 'c', axis=0, tiled=True)  5.86 us
  transfers between devices with their start and end apart: 1, of which 0 were waited for; matrix products, arithmetic and copies ran while one was open for 0% of the time, Pallas kernels for 1%

profile of v3, /device:TPU:1, one launch (start us, length us, event | category | flops | bytes accessed | tf_op | source)
XLA Modules:
  0.0 125.9 jit_solution(13967861009868649251)
XLA Ops:
  1.9 3.3 %front.1 = (bf16[16,40,128]{2,1,0:T(8,128)(2,1)S(1)}, bf16[512,256]{1,0:T(8,128)(2,1)S(1)}, bf16[256,512]{1,0:T(8,128)(2,1)S(1)}, bf16[512,256]{1,0:T(8,128)(2,1...) custom-call(s32[1,1]{1,0:T(1,128)S(6)} %copy.20.rows_ref, ...), custom_call_target="tpu_custom_call" | custom-call | tf_op jit(solution)/shard_map/front/pallas_call | solution.py:353
  5.3 15.8 %all_to_all.35.blocks_ref = bf16[16,40,128]{2,1,0:T(8,128)(2,1)S(1)} all-to-all(bf16[16,40,128]{2,1,0:T(8,128)(2,1)S(1)} %get-tuple-element.52), channel_id=1, replica_groups=mesh['y'=4,'za'=2,'zb'=2,'zc'=2,'zl'=2,'c'=2,'x'=4] {'zl','y','c'}, dimensions={0} | all-to-all | bytes 327680 | tf_op jit(solution)/shard_map/all_to_all | solution.py:398
  21.0 0.3 dense.1
  21.3 0.0 copy-start
  21.3 23.0 %all_to_all.36.sums_ref = bf16[8,40,128]{2,1,0:T(8,128)(2,1)S(1)} all-to-all(bf16[8,40,128]{2,1,0:T(8,128)(2,1)S(1)} %dense.1), channel_id=1, replica_groups=mesh['y'=4,'za'=2,'zb'=2,'zc'=2,'zl'=2,'c'=2,'x'=4] {'zb','zc','za'}, dimensions={0} | all-to-all | bytes 163840 | tf_op jit(solution)/shard_map/all_to_all | solution.py:400
  44.3 0.0 copy-done
  44.3 1.4 %attend.1 = (bf16[8,40,128]{2,1,0:T(8,128)(2,1)S(1)}, f32[64,32]{1,0:T(8,128)S(1)}, f32[64,96]{1,0:T(8,128)S(1)}) custom-call(bf16[8,40,128]{2,1,0:T(8,128)(2,1)S(1)} %all_to_all.36.sums_ref, f32[32,96]{1,0:T(8,128)S(1)} %copy-done), custom_call_target="tpu_custom_call" | custom-call | tf_op jit(solution)/shard_map/attend/pallas_call | solution.py:353
  45.7 15.3 %all_to_all.37.meshes_ref = bf16[8,40,128]{2,1,0:T(8,128)(2,1)S(1)} all-to-all(bf16[8,40,128]{2,1,0:T(8,128)(2,1)S(1)} %get-tuple-element.53), channel_id=1, replica_groups=mesh['y'=4,'za'=2,'zb'=2,'zc'=2,'zl'=2,'c'=2,'x'=4] {'zb','zc','za'}, dimensions={0} | all-to-all | bytes 163840 | tf_op jit(solution)/shard_map/all_to_all | solution.py:407
  61.0 0.2 choose.1
  61.2 12.6 %all_to_all.38.tokens_ref = bf16[16,40,128]{2,1,0:T(8,128)(2,1)S(1)} all-to-all(bf16[16,40,128]{2,1,0:T(8,128)(2,1)S(1)} %choose.1), channel_id=1, replica_groups=mesh['y'=4,'za'=2,'zb'=2,'zc'=2,'zl'=2,'c'=2,'x'=4] {'zl','y','c'}, dimensions={0} | all-to-all | bytes 327680 | tf_op jit(solution)/shard_map/all_to_all | solution.py:409
  73.7 1.9 %back.1 = (bf16[32,24,128]{2,1,0:T(8,128)(2,1)S(1)}, bf16[32,24,128]{2,1,0:T(8,128)(2,1)S(1)}, bf16[256,512]{1,0:T(8,128)(2,1)S(1)}, bf16[256,512]{1,0:T(8,128)(...) custom-call(bf16[512,256]{1,0:T(8,128)(2,1)S(1)} %get-tuple-element.42.normed_ref, ...), custom_call_target="tpu_custom_call" | custom-call | tf_op jit(solution)/shard_map/back/pallas_call | solution.py:353
  75.6 2.7 %collective-permute-start = (bf16[32,24,128]{2,1,0:T(8,128)(2,1)S(1)}, bf16[32,24,128]{2,1,0:T(8,128)(2,1)S(1)}, u32[]{:S(2)}, u32[]{:S(2)}) collective-permute-start(bf16[32,24,128]{2,1,0:T(8,128)(2,1)S(1)} %get-tuple-element.67), channel_id=1, source_target_pairs={{0,4},{4,0},{1,5},{5,1},{2,6},{6,2},{3,7},{7,3},{8,12},{12,8},{9,1... | collective-permute-start | bytes 589832 | tf_op jit(solution)/shard_map/ppermute | solution.py:418
  78.3 1.4 %norm.1 = (bf16[512,256]{1,0:T(8,128)(2,1)}, f32[256,128]{1,0:T(8,128)S(1)}) custom-call(bf16[256,512]{1,0:T(8,128)(2,1)S(1)} %get-tuple-element.54.dmid_ref, bf16[256,512]{1,0:T(8,128)(2,1)S(1)} %get-tuple-element.55.dfeat_ref, bf16[256,256]{1,0:T(8,128)(2,1)S(1)} %get-tuple-element.56.wx_ref, bf16[256,256]{1,0:T(8,128)(2,1)S(1)} %get-tuple-element.57.wfx_ref, ...), custom_call_target="tpu_custom_call" | custom-call | flops 134217728 | bytes 4194304 | tf_op jit(solution)/shard_map/norm/pallas_call | solution.py:353
  79.7 0.0 collective-permute-done.b_ref
  79.7 0.1 add_pair.1
  79.7 12.6 %all_to_all.39.parts_ref = bf16[32,32,128]{2,1,0:T(8,128)(2,1)S(1)} all-to-all(bf16[32,32,128]{2,1,0:T(8,128)(2,1)S(1)} %add_pair.1), channel_id=1, replica_groups=mesh['y'=4,'za'=2,'zb'=2,'zc'=2,'zl'=2,'c'=2,'x'=4] {'y','zl','x'}, dimensions={0} | all-to-all | bytes 524288 | tf_op jit(solution)/shard_map/all_to_all | solution.py:428
  92.4 14.0 %all_to_all.40.parts_ref = bf16[8,32,128]{2,1,0:T(8,128)(2,1)S(1)} all-to-all(bf16[8,32,128]{2,1,0:T(8,128)(2,1)S(1)} %sum_peers.1), channel_id=1, replica_groups=mesh['y'=4,'za'=2,'zb'=2,'zc'=2,'zl'=2,'c'=2,'x'=4] {'zb','zc','za'}, dimensions={0} | all-to-all | bytes 131072 | tf_op jit(solution)/shard_map/all_to_all | solution.py:430
  106.5 12.6 %all_to_all.41 = bf16[32,32,128]{2,1,0:T(8,128)(2,1)S(1)} all-to-all(bf16[32,32,128]{2,1,0:T(8,128)(2,1)S(1)} %sum_z.1), channel_id=1, replica_groups=mesh['y'=4,'za'=2,'zb'=2,'zc'=2,'zl'=2,'c'=2,'x'=4] {'y','zl','x'}, dimensions={0} | all-to-all | bytes 524288 | tf_op jit(solution)/shard_map/all_to_all | solution.py:432
  119.0 5.9 %all_gather.3.parts_ref = bf16[64,32,128]{2,1,0:T(8,128)(2,1)S(1)} all-gather(bf16[32,32,128]{2,1,0:T(8,128)(2,1)S(1)} %all_to_all.41), channel_id=1, replica_groups=mesh['y'=4,'za'=2,'zb'=2,'zc'=2,'zl'=2,'c'=2,'x'=4] {'c'}, dimensions={0}, use_global_device_ids=true | all-gather | bytes 786432 | tf_op jit(solution)/shard_map/all_gather | solution.py:433
  124.9 1.0 finish.1
  (2 shorter events, 0.1 us)
Async XLA Ops:
  21.3 23.0 %copy-start = (f32[32,96]{1,0:T(8,128)S(1)}, f32[32,96]{1,0:T(8,128)}, u32[]{:S(2)}) copy-start(f32[32,96]{1,0:T(8,128)} %qkv_ref.1) | copy-start | bytes 36868
  75.6 4.0 %collective-permute-start = (bf16[32,24,128]{2,1,0:T(8,128)(2,1)S(1)}, bf16[32,24,128]{2,1,0:T(8,128)(2,1)S(1)}, u32[]{:S(2)}, u32[]{:S(2)}) collective-permute-start(bf16[32,24,128]{2,1,0:T(8,128)(2,1)S(1)} %get-tuple-element.67), channel_id=1, source_target_pairs={{0,4},{4,0},{1,5},{5,1},{2,6},{6,2},{3,7},{7,3},{8,12},{12,8},{9,1... | collective-permute-start | bytes 589832 | tf_op jit(solution)/shard_map/ppermute | solution.py:418

commit v4 on v3

--- a/solution.py
+++ b/solution.py
@@ -83,6 +83,10 @@
 
 def row_to_column(row):
     return jnp.sum(jnp.where(eye_mask(), row, 0.0), axis=1, keepdims=True)
+
+
+def low_part(values):
+    return values - values.astype(BF16).astype(F32)
 
 
 def normalise(x):
@@ -154,7 +158,7 @@
     row = iota((8, 128), 0)
     mesh = mesh_ref[0, 0]
     number = jnp.where(row == 1, ((mesh >> 1) + 1).astype(F32), 0.0)
-    tails = [jnp.where(row == 0, mass, number)[None] for mass in masses]
+    tails = [jnp.where(row == 0, mass, jnp.where(row == 2, low_part(mass), number))[None] for mass in masses]
     packed = [jnp.concatenate(tables, axis=0), jnp.concatenate(grads, axis=0), jnp.concatenate(tails, axis=0)]
     packed = jnp.concatenate(packed, axis=1)
     odd = (mesh & 1).astype(F32)
@@ -164,14 +168,18 @@
 def dense_kernel(blocks_ref, out_ref):
     blocks = blocks_ref[...].astype(F32)
     numbers = blocks[:, 33:34, :]
+    row = iota((40, 128), 0)
     for k in range(OWNERS):
-        out_ref[k] = jnp.sum(jnp.where(numbers == float(k + 1), blocks, 0.0), axis=0).astype(BF16)
+        total = jnp.sum(jnp.where(numbers == float(k + 1), blocks, 0.0), axis=0)
+        mass = total[32:33] + total[34:35]
+        total = jnp.where(row == 32, mass, jnp.where(row == 34, low_part(mass), total))
+        out_ref[k] = total.astype(BF16)
 
 
 def attend_kernel(sums_ref, qkv_ref, out_ref, token_ref, d_qkv_ref):
     sums = jnp.sum(sums_ref[...].astype(F32), axis=0)
     w_qkv = qkv_ref[...]
-    mass = row_to_column(sums[32:33, :])
+    mass = row_to_column(sums[32:33, :] + sums[34:35, :])
     inv = 1.0 / (mass + EPS_MASS)
 
     def unfold(spread):
@@ -201,7 +209,9 @@
     def pack(values):
         return pack_rows(jnp.concatenate([values] * 4, axis=1))[0]
 
-    tail = jnp.where(iota((8, 128), 0) == 0, column_to_row(d_mass), 0.0)
+    tail = column_to_row(d_mass)
+    row = iota((8, 128), 0)
+    tail = jnp.where(row == 0, tail, jnp.where(row == 2, low_part(tail), 0.0))
     packed = jnp.concatenate([pack(mixed), pack(d_table), tail], axis=0).astype(BF16)
     out_ref[...] = jnp.broadcast_to(packed[None], (OWNERS, 40, 128))
 
@@ -240,7 +250,7 @@
         wide = slice(group * 256, (group + 1) * 256)
         heads = tokens[4 * group : 4 * group + 4]
         chosen = jnp.concatenate([block_of(heads[:, 0:16]), block_of(heads[:, 16:32])], axis=1)
-        d_mass = jnp.concatenate([row_to_column(heads[i, 32:33, :]) for i in range(4)], axis=0)
+        d_mass = jnp.concatenate([row_to_column(heads[i, 32:33, :] + heads[i, 34:35, :]) for i in range(4)], axis=0)
         pair = dot(chosen, sw_ref[wide, :], ((0,), (0,)))
         outs.append(pair[:128].astype(BF16))
         d_feats.append(pair[128:].astype(BF16))

time: 126 us -> 126 us (level)
  no operation moved by 1% of the time
where the time goes in v4:
time: 126 us
  blocking collectives  112 us (89%)
  Pallas kernels  9.52 us (8%)
  starting transfers between devices  2.62 us (2%)
  between operations  1.98 us (2%)
    all_to_all x2, blocking collectives, shards(): parts = lax.all_to_all(parts, across, 0, 0)  25.2 us
    all_to_all x1, blocking collectives, shards(): sums = lax.all_to_all(dense, ('zb', 'zc', 'za'), 0, 0)  23 us
    all_to_all x1, blocking collectives, shards(): blocks = lax.all_to_all(send, ('zl', 'y', 'c'), 0, 0)  15.8 us
    all_to_all x1, blocking collectives, shards(): meshes = lax.all_to_all(answer, ('zb', 'zc', 'za'), 0, 0)  15.3 us
    all_to_all x1, blocking collectives, shards(): parts = lax.all_to_all(parts, ('zb', 'zc', 'za'), 0, 0)  14 us
    all_to_all x1, blocking collectives, shards(): tokens = lax.all_to_all(chosen, ('zl', 'y', 'c'), 0, 0)  12.6 us
    pallas_call x10, Pallas kernels, call(): pl.pallas_call(kernel, name=name, out_shape=outputs, in_specs=[pl.BlockSp...  9.52 us
    all_gather x1, blocking collectives, shards(): parts = lax.all_gather(parts, 'c', axis=0, tiled=True)  5.86 us
  transfers between devices with their start and end apart: 1, of which 0 were waited for; matrix products, arithmetic and copies ran while one was open for 0% of the time, Pallas kernels for 1%

profile of v4, /device:TPU:1, one launch (start us, length us, event | category | flops | bytes accessed | tf_op | source)
XLA Modules:
  0.0 125.9 jit_solution(10951695510252773877)
XLA Ops:
  1.9 3.3 %front.1 = (bf16[16,40,128]{2,1,0:T(8,128)(2,1)S(1)}, bf16[512,256]{1,0:T(8,128)(2,1)S(1)}, bf16[256,512]{1,0:T(8,128)(2,1)S(1)}, bf16[512,256]{1,0:T(8,128)(2,1...) custom-call(s32[1,1]{1,0:T(1,128)S(6)} %copy.20.rows_ref, ...), custom_call_target="tpu_custom_call" | custom-call | tf_op jit(solution)/shard_map/front/pallas_call | solution.py:363
  5.3 15.8 %all_to_all.35.blocks_ref = bf16[16,40,128]{2,1,0:T(8,128)(2,1)S(1)} all-to-all(bf16[16,40,128]{2,1,0:T(8,128)(2,1)S(1)} %get-tuple-element.52), channel_id=1, replica_groups=mesh['y'=4,'za'=2,'zb'=2,'zc'=2,'zl'=2,'c'=2,'x'=4] {'zl','y','c'}, dimensions={0} | all-to-all | bytes 327680 | tf_op jit(solution)/shard_map/all_to_all | solution.py:408
  21.0 0.3 dense.1
  21.3 0.0 copy-start
  21.3 23.0 %all_to_all.36.sums_ref = bf16[8,40,128]{2,1,0:T(8,128)(2,1)S(1)} all-to-all(bf16[8,40,128]{2,1,0:T(8,128)(2,1)S(1)} %dense.1), channel_id=1, replica_groups=mesh['y'=4,'za'=2,'zb'=2,'zc'=2,'zl'=2,'c'=2,'x'=4] {'zb','zc','za'}, dimensions={0} | all-to-all | bytes 163840 | tf_op jit(solution)/shard_map/all_to_all | solution.py:410
  44.3 0.0 copy-done
  44.3 1.4 %attend.1 = (bf16[8,40,128]{2,1,0:T(8,128)(2,1)S(1)}, f32[64,32]{1,0:T(8,128)S(1)}, f32[64,96]{1,0:T(8,128)S(1)}) custom-call(bf16[8,40,128]{2,1,0:T(8,128)(2,1)S(1)} %all_to_all.36.sums_ref, f32[32,96]{1,0:T(8,128)S(1)} %copy-done), custom_call_target="tpu_custom_call" | custom-call | tf_op jit(solution)/shard_map/attend/pallas_call | solution.py:363
  45.7 15.3 %all_to_all.37.meshes_ref = bf16[8,40,128]{2,1,0:T(8,128)(2,1)S(1)} all-to-all(bf16[8,40,128]{2,1,0:T(8,128)(2,1)S(1)} %get-tuple-element.53), channel_id=1, replica_groups=mesh['y'=4,'za'=2,'zb'=2,'zc'=2,'zl'=2,'c'=2,'x'=4] {'zb','zc','za'}, dimensions={0} | all-to-all | bytes 163840 | tf_op jit(solution)/shard_map/all_to_all | solution.py:417
  61.0 0.2 choose.1
  61.2 12.6 %all_to_all.38.tokens_ref = bf16[16,40,128]{2,1,0:T(8,128)(2,1)S(1)} all-to-all(bf16[16,40,128]{2,1,0:T(8,128)(2,1)S(1)} %choose.1), channel_id=1, replica_groups=mesh['y'=4,'za'=2,'zb'=2,'zc'=2,'zl'=2,'c'=2,'x'=4] {'zl','y','c'}, dimensions={0} | all-to-all | bytes 327680 | tf_op jit(solution)/shard_map/all_to_all | solution.py:419
  73.8 1.9 %back.1 = (bf16[32,24,128]{2,1,0:T(8,128)(2,1)S(1)}, bf16[32,24,128]{2,1,0:T(8,128)(2,1)S(1)}, bf16[256,512]{1,0:T(8,128)(2,1)S(1)}, bf16[256,512]{1,0:T(8,128)(...) custom-call(bf16[512,256]{1,0:T(8,128)(2,1)S(1)} %get-tuple-element.42.normed_ref, ...), custom_call_target="tpu_custom_call" | custom-call | tf_op jit(solution)/shard_map/back/pallas_call | solution.py:363
  75.7 2.6 %collective-permute-start = (bf16[32,24,128]{2,1,0:T(8,128)(2,1)S(1)}, bf16[32,24,128]{2,1,0:T(8,128)(2,1)S(1)}, u32[]{:S(2)}, u32[]{:S(2)}) collective-permute-start(bf16[32,24,128]{2,1,0:T(8,128)(2,1)S(1)} %get-tuple-element.67), channel_id=1, source_target_pairs={{0,4},{4,0},{1,5},{5,1},{2,6},{6,2},{3,7},{7,3},{8,12},{12,8},{9,1... | collective-permute-start | bytes 589832 | tf_op jit(solution)/shard_map/ppermute | solution.py:428
  78.3 1.4 %norm.1 = (bf16[512,256]{1,0:T(8,128)(2,1)}, f32[256,128]{1,0:T(8,128)S(1)}) custom-call(bf16[256,512]{1,0:T(8,128)(2,1)S(1)} %get-tuple-element.54.dmid_ref, bf16[256,512]{1,0:T(8,128)(2,1)S(1)} %get-tuple-element.55.dfeat_ref, bf16[256,256]{1,0:T(8,128)(2,1)S(1)} %get-tuple-element.56.wx_ref, bf16[256,256]{1,0:T(8,128)(2,1)S(1)} %get-tuple-element.57.wfx_ref, ...), custom_call_target="tpu_custom_call" | custom-call | flops 134217728 | bytes 4194304 | tf_op jit(solution)/shard_map/norm/pallas_call | solution.py:363
  79.7 0.0 collective-permute-done.b_ref
  79.7 0.1 add_pair.1
  79.7 12.7 %all_to_all.39.parts_ref = bf16[32,32,128]{2,1,0:T(8,128)(2,1)S(1)} all-to-all(bf16[32,32,128]{2,1,0:T(8,128)(2,1)S(1)} %add_pair.1), channel_id=1, replica_groups=mesh['y'=4,'za'=2,'zb'=2,'zc'=2,'zl'=2,'c'=2,'x'=4] {'y','zl','x'}, dimensions={0} | all-to-all | bytes 524288 | tf_op jit(solution)/shard_map/all_to_all | solution.py:438
  92.4 14.0 %all_to_all.40.parts_ref = bf16[8,32,128]{2,1,0:T(8,128)(2,1)S(1)} all-to-all(bf16[8,32,128]{2,1,0:T(8,128)(2,1)S(1)} %sum_peers.1), channel_id=1, replica_groups=mesh['y'=4,'za'=2,'zb'=2,'zc'=2,'zl'=2,'c'=2,'x'=4] {'zb','zc','za'}, dimensions={0} | all-to-all | bytes 131072 | tf_op jit(solution)/shard_map/all_to_all | solution.py:440
  106.5 12.6 %all_to_all.41 = bf16[32,32,128]{2,1,0:T(8,128)(2,1)S(1)} all-to-all(bf16[32,32,128]{2,1,0:T(8,128)(2,1)S(1)} %sum_z.1), channel_id=1, replica_groups=mesh['y'=4,'za'=2,'zb'=2,'zc'=2,'zl'=2,'c'=2,'x'=4] {'y','zl','x'}, dimensions={0} | all-to-all | bytes 524288 | tf_op jit(solution)/shard_map/all_to_all | solution.py:442
  119.0 5.9 %all_gather.3.parts_ref = bf16[64,32,128]{2,1,0:T(8,128)(2,1)S(1)} all-gather(bf16[32,32,128]{2,1,0:T(8,128)(2,1)S(1)} %all_to_all.41), channel_id=1, replica_groups=mesh['y'=4,'za'=2,'zb'=2,'zc'=2,'zl'=2,'c'=2,'x'=4] {'c'}, dimensions={0}, use_global_device_ids=true | all-gather | bytes 786432 | tf_op jit(solution)/shard_map/all_gather | solution.py:443
  124.9 1.0 finish.1
  (2 shorter events, 0.1 us)
Async XLA Ops:
  21.3 23.0 %copy-start = (f32[32,96]{1,0:T(8,128)S(1)}, f32[32,96]{1,0:T(8,128)}, u32[]{:S(2)}) copy-start(f32[32,96]{1,0:T(8,128)} %qkv_ref.1) | copy-start | bytes 36868
  75.7 4.0 %collective-permute-start = (bf16[32,24,128]{2,1,0:T(8,128)(2,1)S(1)}, bf16[32,24,128]{2,1,0:T(8,128)(2,1)S(1)}, u32[]{:S(2)}, u32[]{:S(2)}) collective-permute-start(bf16[32,24,128]{2,1,0:T(8,128)(2,1)S(1)} %get-tuple-element.67), channel_id=1, source_target_pairs={{0,4},{4,0},{1,5},{5,1},{2,6},{6,2},{3,7},{7,3},{8,12},{12,8},{9,1... | collective-permute-start | bytes 589832 | tf_op jit(solution)/shard_map/ppermute | solution.py:428

commit v5 on v4

--- a/solution.py
+++ b/solution.py
@@ -113,24 +113,19 @@
     xhat, rstd = normalise(x_ref[...])
     xhat_ref[...] = xhat
     rstd_ref[...] = rstd
-    copies[1].wait()
+    for copy in copies[1:]:
+        copy.wait()
     normed = (xhat * gain_ref[...]).astype(BF16)
     normed_ref[...] = normed
-    copies[2].wait()
     mid = dot(wx_ref[...], normed, ((0,), (1,))).astype(BF16)
-    copies[3].wait()
     feat = dot(normed, wfx_ref[...]).astype(BF16)
     mid_ref[...] = mid
     feat_ref[...] = feat
-    copies[4].wait()
     blocks = four_blocks(slice_ref[...])
     blocks_ref[...] = blocks
-    copies[5].wait()
     heat = heat_ref[...]
-    copies[6].wait()
     g_b = jnp.where(iota((ROWS, 1), 0) < rows_ref[0, 0], cot_ref[...].astype(F32), 0.0).astype(BF16)
     g_ref[...] = g_b
-    copies[7].wait()
     d_out = dot(g_b, wout_ref[...], ((1,), (1,))).astype(BF16)
     dout_ref[...] = d_out
     fold = fold_matrix()

time: 126 us -> 126 us (level)
  no operation moved by 1% of the time
where the time goes in v5:
time: 126 us; the launch traced here: 125 us
  blocking collectives  112 us (89%)
  Pallas kernels  8.9 us (7%)
  starting transfers between devices  2.63 us (2%)
  between operations  1.98 us (2%)
    all_to_all x2, blocking collectives, shards(): parts = lax.all_to_all(parts, across, 0, 0)  25.2 us
    all_to_all x1, blocking collectives, shards(): sums = lax.all_to_all(dense, ('zb', 'zc', 'za'), 0, 0)  23 us
    all_to_all x1, blocking collectives, shards(): blocks = lax.all_to_all(send, ('zl', 'y', 'c'), 0, 0)  15.8 us
    all_to_all x1, blocking collectives, shards(): meshes = lax.all_to_all(answer, ('zb', 'zc', 'za'), 0, 0)  15.3 us
    all_to_all x1, blocking collectives, shards(): parts = lax.all_to_all(parts, ('zb', 'zc', 'za'), 0, 0)  14 us
    all_to_all x1, blocking collectives, shards(): tokens = lax.all_to_all(chosen, ('zl', 'y', 'c'), 0, 0)  12.6 us
    pallas_call x10, Pallas kernels, call(): pl.pallas_call(kernel, name=name, out_shape=outputs, in_specs=[pl.BlockSp...  8.9 us
    all_gather x1, blocking collectives, shards(): parts = lax.all_gather(parts, 'c', axis=0, tiled=True)  5.86 us
  transfers between devices with their start and end apart: 1, of which 0 were waited for; matrix products, arithmetic and copies ran while one was open for 0% of the time, Pallas kernels for 1%

profile of v5, /device:TPU:1, one launch (start us, length us, event | category | flops | bytes accessed | tf_op | source)
XLA Modules:
  0.0 125.2 jit_solution(5567121223166417289)
XLA Ops:
  1.9 2.7 %front.1 = (bf16[16,40,128]{2,1,0:T(8,128)(2,1)S(1)}, bf16[512,256]{1,0:T(8,128)(2,1)S(1)}, bf16[256,512]{1,0:T(8,128)(2,1)S(1)}, bf16[512,256]{1,0:T(8,128)(2,1...) custom-call(s32[1,1]{1,0:T(1,128)S(6)} %copy.20.rows_ref, ...), custom_call_target="tpu_custom_call" | custom-call | tf_op jit(solution)/shard_map/front/pallas_call | solution.py:358
  4.6 15.8 %all_to_all.35.blocks_ref = bf16[16,40,128]{2,1,0:T(8,128)(2,1)S(1)} all-to-all(bf16[16,40,128]{2,1,0:T(8,128)(2,1)S(1)} %get-tuple-element.52), channel_id=1, replica_groups=mesh['y'=4,'za'=2,'zb'=2,'zc'=2,'zl'=2,'c'=2,'x'=4] {'zl','y','c'}, dimensions={0} | all-to-all | bytes 327680 | tf_op jit(solution)/shard_map/all_to_all | solution.py:403
  20.4 0.3 dense.1
  20.7 0.0 copy-start
  20.7 23.0 %all_to_all.36.sums_ref = bf16[8,40,128]{2,1,0:T(8,128)(2,1)S(1)} all-to-all(bf16[8,40,128]{2,1,0:T(8,128)(2,1)S(1)} %dense.1), channel_id=1, replica_groups=mesh['y'=4,'za'=2,'zb'=2,'zc'=2,'zl'=2,'c'=2,'x'=4] {'zb','zc','za'}, dimensions={0} | all-to-all | bytes 163840 | tf_op jit(solution)/shard_map/all_to_all | solution.py:405
  43.7 0.0 copy-done
  43.7 1.4 %attend.1 = (bf16[8,40,128]{2,1,0:T(8,128)(2,1)S(1)}, f32[64,32]{1,0:T(8,128)S(1)}, f32[64,96]{1,0:T(8,128)S(1)}) custom-call(bf16[8,40,128]{2,1,0:T(8,128)(2,1)S(1)} %all_to_all.36.sums_ref, f32[32,96]{1,0:T(8,128)S(1)} %copy-done), custom_call_target="tpu_custom_call" | custom-call | tf_op jit(solution)/shard_map/attend/pallas_call | solution.py:358
  45.1 15.3 %all_to_all.37.meshes_ref = bf16[8,40,128]{2,1,0:T(8,128)(2,1)S(1)} all-to-all(bf16[8,40,128]{2,1,0:T(8,128)(2,1)S(1)} %get-tuple-element.53), channel_id=1, replica_groups=mesh['y'=4,'za'=2,'zb'=2,'zc'=2,'zl'=2,'c'=2,'x'=4] {'zb','zc','za'}, dimensions={0} | all-to-all | bytes 163840 | tf_op jit(solution)/shard_map/all_to_all | solution.py:412
  60.4 0.2 choose.1
  60.5 12.6 %all_to_all.38.tokens_ref = bf16[16,40,128]{2,1,0:T(8,128)(2,1)S(1)} all-to-all(bf16[16,40,128]{2,1,0:T(8,128)(2,1)S(1)} %choose.1), channel_id=1, replica_groups=mesh['y'=4,'za'=2,'zb'=2,'zc'=2,'zl'=2,'c'=2,'x'=4] {'zl','y','c'}, dimensions={0} | all-to-all | bytes 327680 | tf_op jit(solution)/shard_map/all_to_all | solution.py:414
  73.1 1.9 %back.1 = (bf16[32,24,128]{2,1,0:T(8,128)(2,1)S(1)}, bf16[32,24,128]{2,1,0:T(8,128)(2,1)S(1)}, bf16[256,512]{1,0:T(8,128)(2,1)S(1)}, bf16[256,512]{1,0:T(8,128)(...) custom-call(bf16[512,256]{1,0:T(8,128)(2,1)S(1)} %get-tuple-element.42.normed_ref, ...), custom_call_target="tpu_custom_call" | custom-call | tf_op jit(solution)/shard_map/back/pallas_call | solution.py:358
  75.0 2.6 %collective-permute-start = (bf16[32,24,128]{2,1,0:T(8,128)(2,1)S(1)}, bf16[32,24,128]{2,1,0:T(8,128)(2,1)S(1)}, u32[]{:S(2)}, u32[]{:S(2)}) collective-permute-start(bf16[32,24,128]{2,1,0:T(8,128)(2,1)S(1)} %get-tuple-element.67), channel_id=1, source_target_pairs={{0,4},{4,0},{1,5},{5,1},{2,6},{6,2},{3,7},{7,3},{8,12},{12,8},{9,1... | collective-permute-start | bytes 589832 | tf_op jit(solution)/shard_map/ppermute | solution.py:423
  77.7 1.4 %norm.1 = (bf16[512,256]{1,0:T(8,128)(2,1)}, f32[256,128]{1,0:T(8,128)S(1)}) custom-call(bf16[256,512]{1,0:T(8,128)(2,1)S(1)} %get-tuple-element.54.dmid_ref, bf16[256,512]{1,0:T(8,128)(2,1)S(1)} %get-tuple-element.55.dfeat_ref, bf16[256,256]{1,0:T(8,128)(2,1)S(1)} %get-tuple-element.56.wx_ref, bf16[256,256]{1,0:T(8,128)(2,1)S(1)} %get-tuple-element.57.wfx_ref, ...), custom_call_target="tpu_custom_call" | custom-call | flops 134217728 | bytes 4194304 | tf_op jit(solution)/shard_map/norm/pallas_call | solution.py:358
  79.0 0.0 collective-permute-done.b_ref
  79.0 0.1 add_pair.1
  79.1 12.6 %all_to_all.39.parts_ref = bf16[32,32,128]{2,1,0:T(8,128)(2,1)S(1)} all-to-all(bf16[32,32,128]{2,1,0:T(8,128)(2,1)S(1)} %add_pair.1), channel_id=1, replica_groups=mesh['y'=4,'za'=2,'zb'=2,'zc'=2,'zl'=2,'c'=2,'x'=4] {'y','zl','x'}, dimensions={0} | all-to-all | bytes 524288 | tf_op jit(solution)/shard_map/all_to_all | solution.py:433
  91.8 14.0 %all_to_all.40.parts_ref = bf16[8,32,128]{2,1,0:T(8,128)(2,1)S(1)} all-to-all(bf16[8,32,128]{2,1,0:T(8,128)(2,1)S(1)} %sum_peers.1), channel_id=1, replica_groups=mesh['y'=4,'za'=2,'zb'=2,'zc'=2,'zl'=2,'c'=2,'x'=4] {'zb','zc','za'}, dimensions={0} | all-to-all | bytes 131072 | tf_op jit(solution)/shard_map/all_to_all | solution.py:435
  105.9 12.6 %all_to_all.41 = bf16[32,32,128]{2,1,0:T(8,128)(2,1)S(1)} all-to-all(bf16[32,32,128]{2,1,0:T(8,128)(2,1)S(1)} %sum_z.1), channel_id=1, replica_groups=mesh['y'=4,'za'=2,'zb'=2,'zc'=2,'zl'=2,'c'=2,'x'=4] {'y','zl','x'}, dimensions={0} | all-to-all | bytes 524288 | tf_op jit(solution)/shard_map/all_to_all | solution.py:437
  118.4 5.9 %all_gather.3.parts_ref = bf16[64,32,128]{2,1,0:T(8,128)(2,1)S(1)} all-gather(bf16[32,32,128]{2,1,0:T(8,128)(2,1)S(1)} %all_to_all.41), channel_id=1, replica_groups=mesh['y'=4,'za'=2,'zb'=2,'zc'=2,'zl'=2,'c'=2,'x'=4] {'c'}, dimensions={0}, use_global_device_ids=true | all-gather | bytes 786432 | tf_op jit(solution)/shard_map/all_gather | solution.py:438
  124.3 1.0 finish.1
  (2 shorter events, 0.1 us)
Async XLA Ops:
  20.7 23.0 %copy-start = (f32[32,96]{1,0:T(8,128)S(1)}, f32[32,96]{1,0:T(8,128)}, u32[]{:S(2)}) copy-start(f32[32,96]{1,0:T(8,128)} %qkv_ref.1) | copy-start | bytes 36868
  75.0 4.0 %collective-permute-start = (bf16[32,24,128]{2,1,0:T(8,128)(2,1)S(1)}, bf16[32,24,128]{2,1,0:T(8,128)(2,1)S(1)}, u32[]{:S(2)}, u32[]{:S(2)}) collective-permute-start(bf16[32,24,128]{2,1,0:T(8,128)(2,1)S(1)} %get-tuple-element.67), channel_id=1, source_target_pairs={{0,4},{4,0},{1,5},{5,1},{2,6},{6,2},{3,7},{7,3},{8,12},{12,8},{9,1... | collective-permute-start | bytes 589832 | tf_op jit(solution)/shard_map/ppermute | solution.py:423

commit v6 on v5

--- a/solution.py
+++ b/solution.py
@@ -328,7 +328,6 @@
 
     def leave(source, target):
         copies.append(pltpu.make_async_copy(source, target, sems.at[len(copies)]))
-        copies[-1].start()
 
     for at, (ref, hbm) in enumerate(((out_ref, out_hbm), (in_x_ref, in_x_hbm), (in_fx_ref, in_fx_hbm))):
         for half in range(2):
@@ -347,6 +346,8 @@
     leave(gain_ref, gain_hbm)
     temper_ref[...] = small[66:67, :8]
     leave(temper_ref, temper_hbm)
+    for copy in copies:
+        copy.start()
     for copy in copies:
         copy.wait()
 

time: 126 us -> 126 us (level)
  no operation moved by 1% of the time
where the time goes in v6:
time: 126 us; the launch traced here: 125 us
  blocking collectives  112 us (89%)
  Pallas kernels  8.9 us (7%)
  starting transfers between devices  2.63 us (2%)
  between operations  1.98 us (2%)
    all_to_all x2, blocking collectives, shards(): parts = lax.all_to_all(parts, across, 0, 0)  25.2 us
    all_to_all x1, blocking collectives, shards(): sums = lax.all_to_all(dense, ('zb', 'zc', 'za'), 0, 0)  23 us
    all_to_all x1, blocking collectives, shards(): blocks = lax.all_to_all(send, ('zl', 'y', 'c'), 0, 0)  15.8 us
    all_to_all x1, blocking collectives, shards(): meshes = lax.all_to_all(answer, ('zb', 'zc', 'za'), 0, 0)  15.3 us
    all_to_all x1, blocking collectives, shards(): parts = lax.all_to_all(parts, ('zb', 'zc', 'za'), 0, 0)  14 us
    all_to_all x1, blocking collectives, shards(): tokens = lax.all_to_all(chosen, ('zl', 'y', 'c'), 0, 0)  12.6 us
    pallas_call x10, Pallas kernels, call(): pl.pallas_call(kernel, name=name, out_shape=outputs, in_specs=[pl.BlockSp...  8.9 us
    all_gather x1, blocking collectives, shards(): parts = lax.all_gather(parts, 'c', axis=0, tiled=True)  5.86 us
  transfers between devices with their start and end apart: 1, of which 0 were waited for; matrix products, arithmetic and copies ran while one was open for 0% of the time, Pallas kernels for 1%

profile of v6, /device:TPU:1, one launch (start us, length us, event | category | flops | bytes accessed | tf_op | source)
XLA Modules:
  0.0 125.2 jit_solution(5567121223166417289)
XLA Ops:
  1.9 2.7 %front.1 = (bf16[16,40,128]{2,1,0:T(8,128)(2,1)S(1)}, bf16[512,256]{1,0:T(8,128)(2,1)S(1)}, bf16[256,512]{1,0:T(8,128)(2,1)S(1)}, bf16[512,256]{1,0:T(8,128)(2,1...) custom-call(s32[1,1]{1,0:T(1,128)S(6)} %copy.20.rows_ref, ...), custom_call_target="tpu_custom_call" | custom-call | tf_op jit(solution)/shard_map/front/pallas_call | solution.py:359
  4.6 15.8 %all_to_all.35.blocks_ref = bf16[16,40,128]{2,1,0:T(8,128)(2,1)S(1)} all-to-all(bf16[16,40,128]{2,1,0:T(8,128)(2,1)S(1)} %get-tuple-element.52), channel_id=1, replica_groups=mesh['y'=4,'za'=2,'zb'=2,'zc'=2,'zl'=2,'c'=2,'x'=4] {'zl','y','c'}, dimensions={0} | all-to-all | bytes 327680 | tf_op jit(solution)/shard_map/all_to_all | solution.py:404
  20.4 0.3 dense.1
  20.7 0.0 copy-start
  20.7 23.0 %all_to_all.36.sums_ref = bf16[8,40,128]{2,1,0:T(8,128)(2,1)S(1)} all-to-all(bf16[8,40,128]{2,1,0:T(8,128)(2,1)S(1)} %dense.1), channel_id=1, replica_groups=mesh['y'=4,'za'=2,'zb'=2,'zc'=2,'zl'=2,'c'=2,'x'=4] {'zb','zc','za'}, dimensions={0} | all-to-all | bytes 163840 | tf_op jit(solution)/shard_map/all_to_all | solution.py:406
  43.7 0.0 copy-done
  43.7 1.4 %attend.1 = (bf16[8,40,128]{2,1,0:T(8,128)(2,1)S(1)}, f32[64,32]{1,0:T(8,128)S(1)}, f32[64,96]{1,0:T(8,128)S(1)}) custom-call(bf16[8,40,128]{2,1,0:T(8,128)(2,1)S(1)} %all_to_all.36.sums_ref, f32[32,96]{1,0:T(8,128)S(1)} %copy-done), custom_call_target="tpu_custom_call" | custom-call | tf_op jit(solution)/shard_map/attend/pallas_call | solution.py:359
  45.1 15.3 %all_to_all.37.meshes_ref = bf16[8,40,128]{2,1,0:T(8,128)(2,1)S(1)} all-to-all(bf16[8,40,128]{2,1,0:T(8,128)(2,1)S(1)} %get-tuple-element.53), channel_id=1, replica_groups=mesh['y'=4,'za'=2,'zb'=2,'zc'=2,'zl'=2,'c'=2,'x'=4] {'zb','zc','za'}, dimensions={0} | all-to-all | bytes 163840 | tf_op jit(solution)/shard_map/all_to_all | solution.py:413
  60.4 0.2 choose.1
  60.5 12.6 %all_to_all.38.tokens_ref = bf16[16,40,128]{2,1,0:T(8,128)(2,1)S(1)} all-to-all(bf16[16,40,128]{2,1,0:T(8,128)(2,1)S(1)} %choose.1), channel_id=1, replica_groups=mesh['y'=4,'za'=2,'zb'=2,'zc'=2,'zl'=2,'c'=2,'x'=4] {'zl','y','c'}, dimensions={0} | all-to-all | bytes 327680 | tf_op jit(solution)/shard_map/all_to_all | solution.py:415
  73.1 1.9 %back.1 = (bf16[32,24,128]{2,1,0:T(8,128)(2,1)S(1)}, bf16[32,24,128]{2,1,0:T(8,128)(2,1)S(1)}, bf16[256,512]{1,0:T(8,128)(2,1)S(1)}, bf16[256,512]{1,0:T(8,128)(...) custom-call(bf16[512,256]{1,0:T(8,128)(2,1)S(1)} %get-tuple-element.42.normed_ref, ...), custom_call_target="tpu_custom_call" | custom-call | tf_op jit(solution)/shard_map/back/pallas_call | solution.py:359
  75.0 2.6 %collective-permute-start = (bf16[32,24,128]{2,1,0:T(8,128)(2,1)S(1)}, bf16[32,24,128]{2,1,0:T(8,128)(2,1)S(1)}, u32[]{:S(2)}, u32[]{:S(2)}) collective-permute-start(bf16[32,24,128]{2,1,0:T(8,128)(2,1)S(1)} %get-tuple-element.67), channel_id=1, source_target_pairs={{0,4},{4,0},{1,5},{5,1},{2,6},{6,2},{3,7},{7,3},{8,12},{12,8},{9,1... | collective-permute-start | bytes 589832 | tf_op jit(solution)/shard_map/ppermute | solution.py:424
  77.7 1.4 %norm.1 = (bf16[512,256]{1,0:T(8,128)(2,1)}, f32[256,128]{1,0:T(8,128)S(1)}) custom-call(bf16[256,512]{1,0:T(8,128)(2,1)S(1)} %get-tuple-element.54.dmid_ref, bf16[256,512]{1,0:T(8,128)(2,1)S(1)} %get-tuple-element.55.dfeat_ref, bf16[256,256]{1,0:T(8,128)(2,1)S(1)} %get-tuple-element.56.wx_ref, bf16[256,256]{1,0:T(8,128)(2,1)S(1)} %get-tuple-element.57.wfx_ref, ...), custom_call_target="tpu_custom_call" | custom-call | flops 134217728 | bytes 4194304 | tf_op jit(solution)/shard_map/norm/pallas_call | solution.py:359
  79.0 0.0 collective-permute-done.b_ref
  79.0 0.1 add_pair.1
  79.1 12.6 %all_to_all.39.parts_ref = bf16[32,32,128]{2,1,0:T(8,128)(2,1)S(1)} all-to-all(bf16[32,32,128]{2,1,0:T(8,128)(2,1)S(1)} %add_pair.1), channel_id=1, replica_groups=mesh['y'=4,'za'=2,'zb'=2,'zc'=2,'zl'=2,'c'=2,'x'=4] {'y','zl','x'}, dimensions={0} | all-to-all | bytes 524288 | tf_op jit(solution)/shard_map/all_to_all | solution.py:434
  91.8 14.0 %all_to_all.40.parts_ref = bf16[8,32,128]{2,1,0:T(8,128)(2,1)S(1)} all-to-all(bf16[8,32,128]{2,1,0:T(8,128)(2,1)S(1)} %sum_peers.1), channel_id=1, replica_groups=mesh['y'=4,'za'=2,'zb'=2,'zc'=2,'zl'=2,'c'=2,'x'=4] {'zb','zc','za'}, dimensions={0} | all-to-all | bytes 131072 | tf_op jit(solution)/shard_map/all_to_all | solution.py:436
  105.9 12.6 %all_to_all.41 = bf16[32,32,128]{2,1,0:T(8,128)(2,1)S(1)} all-to-all(bf16[32,32,128]{2,1,0:T(8,128)(2,1)S(1)} %sum_z.1), channel_id=1, replica_groups=mesh['y'=4,'za'=2,'zb'=2,'zc'=2,'zl'=2,'c'=2,'x'=4] {'y','zl','x'}, dimensions={0} | all-to-all | bytes 524288 | tf_op jit(solution)/shard_map/all_to_all | solution.py:438
  118.4 5.9 %all_gather.3.parts_ref = bf16[64,32,128]{2,1,0:T(8,128)(2,1)S(1)} all-gather(bf16[32,32,128]{2,1,0:T(8,128)(2,1)S(1)} %all_to_all.41), channel_id=1, replica_groups=mesh['y'=4,'za'=2,'zb'=2,'zc'=2,'zl'=2,'c'=2,'x'=4] {'c'}, dimensions={0}, use_global_device_ids=true | all-gather | bytes 786432 | tf_op jit(solution)/shard_map/all_gather | solution.py:439
  124.3 1.0 finish.1
  (2 shorter events, 0.1 us)
Async XLA Ops:
  20.7 23.0 %copy-start = (f32[32,96]{1,0:T(8,128)S(1)}, f32[32,96]{1,0:T(8,128)}, u32[]{:S(2)}) copy-start(f32[32,96]{1,0:T(8,128)} %qkv_ref.1) | copy-start | bytes 36868
  75.0 4.0 %collective-permute-start = (bf16[32,24,128]{2,1,0:T(8,128)(2,1)S(1)}, bf16[32,24,128]{2,1,0:T(8,128)(2,1)S(1)}, u32[]{:S(2)}, u32[]{:S(2)}) collective-permute-start(bf16[32,24,128]{2,1,0:T(8,128)(2,1)S(1)} %get-tuple-element.67), channel_id=1, source_target_pairs={{0,4},{4,0},{1,5},{5,1},{2,6},{6,2},{3,7},{7,3},{8,12},{12,8},{9,1... | collective-permute-start | bytes 589832 | tf_op jit(solution)/shard_map/ppermute | solution.py:424
